TPU v7x, 32 devices: a whole 2x2x4 slice. The times are simulated.
32 devices in a mesh: pb: 4 (over y, x), kv: 4 (over z), ha: 2 (over core).
Axes of the slice: x: 2, y: 2, z: 4, core: 2. Of those that a mesh axis runs over, the one named last changes fastest.
Arguments:
- teacher_q: bfloat16 [2048, 4096], P(('pb', 'kv'), 'ha'), may hold values from -240 to 240
- teacher_k: bfloat16 [2048, 1024], P(('pb', 'kv'), 'ha'), may hold values from -6 to 6
- teacher_v: bfloat16 [2048, 1024], P(('pb', 'kv'), 'ha'), may hold values from -6 to 6
- student_q: bfloat16 [2048, 2048], P(('pb', 'kv'), 'ha'), may hold values from -240 to 240
- student_k: bfloat16 [2048, 512], P(('pb', 'kv'), 'ha'), may hold values from -6 to 6
- student_v: bfloat16 [2048, 512], P(('pb', 'kv'), 'ha'), may hold values from -6 to 6
- doc_ids: int32 [2048], P(('pb', 'kv')), may hold values from 0 to 3, never falling along the last dimension, each value on 1 to 1536 neighbouring positions
- proj_weight: bfloat16 [32, 64, 128], replicated, may hold values from -0.75 to 0.75
Outputs:
- grad_w: float32 [2048, 128], P(('pb', 'kv', 'ha'))
- token_loss: float32 [2048], P(('pb', 'kv', 'ha'))
Inputs may be any that keep to these rules, and one draw needn't show every extreme that they name: `doc_ids`: document numbers never fall along the sequence; each document spans 1 to 1536 tokens, and one spans exactly that many.
All inputs are finite; a program needn't handle non-finite values.
Results may differ from a plain program's by a relative error of at most 0.0035.
Values may be sent and summed in bfloat16 or wider, within the bound.
A program may use at most 128 MiB of HBM per device.

v0:
```python
import math

import jax
import jax.numpy as jnp
from jax import lax
from jax.sharding import PartitionSpec as P

TD = 128
SD = 64


NEGATIVE = -1e30
EPSILON = 1e-06


def start_state(queries, head_size, groups):
    queried = queries.shape[0]
    per_group = queries.shape[1] // (groups * head_size)
    largest = jnp.full((groups, per_group, queried), NEGATIVE, jnp.float32)
    totals = jnp.zeros((groups, per_group, queried), jnp.float32)
    accum = jnp.zeros((groups, per_group, queried, head_size), jnp.float32)
    return (largest, totals, accum)


def attend_keys(
    state, queries, query_pos, query_doc, keys_piece, values_piece, key_pos, key_doc, head_size
):
    length = keys_piece.shape[0]
    block = math.gcd(length, 512)
    blocks = length // block
    groups = keys_piece.shape[1] // head_size
    queried = queries.shape[0]
    per_group = queries.shape[1] // (groups * head_size)
    shaped = queries.reshape(queried, groups, per_group, head_size)
    scale = 1.0 / math.sqrt(head_size)
    newest = jnp.max(query_pos)

    def compute(current, key_block, value_block, pos_block, doc_block):
        largest, totals, accum = current
        scores = (
            jnp.einsum(
                "qgpd,kgd->gpqk",
                shaped,
                key_block.reshape(block, groups, head_size),
                preferred_element_type=jnp.float32,
            )
            * scale
        )
        allowed = (query_doc[:, None] == doc_block[None, :]) & (
            pos_block[None, :] <= query_pos[:, None]
        )
        scores = jnp.where(allowed, scores, NEGATIVE)
        updated = jnp.maximum(largest, jnp.max(scores, axis=-1))
        weights = jnp.where(allowed, jnp.exp(scores - updated[..., None]), 0.0)
        factor = jnp.exp(largest - updated)
        totals = totals * factor + jnp.sum(weights, axis=-1)
        mixed = jnp.einsum(
            "gpqk,kgd->gpqd",
            weights.astype(jnp.bfloat16),
            value_block.reshape(block, groups, head_size),
            preferred_element_type=jnp.float32,
        )
        return (updated, totals, accum * factor[..., None] + mixed)

    def visit(current, item):
        key_block, value_block, pos_block, doc_block = item
        result = lax.cond(
            pos_block[0] <= newest,
            lambda inner: compute(inner, key_block, value_block, pos_block, doc_block),
            lambda inner: inner,
            current,
        )
        return (result, None)

    items = (
        keys_piece.reshape(blocks, block, -1),
        values_piece.reshape(blocks, block, -1),
        key_pos.reshape(blocks, block),
        key_doc.reshape(blocks, block),
    )
    final, unused = lax.scan(visit, state, items)
    return final


def finish(totals, accum):
    queried = accum.shape[2]
    result = accum / totals[..., None]
    return jnp.transpose(result, (2, 0, 1, 3)).reshape(queried, -1).astype(jnp.bfloat16)


def local(teacher_q, teacher_k, teacher_v, student_q, student_k, student_v, doc_ids, proj_weight):
    shard_rows = teacher_q.shape[0]
    groups = teacher_k.shape[1] // TD
    outer = lax.axis_size("pb")
    inner_size = lax.axis_size("kv")
    total_tokens = shard_rows * outer * inner_size
    shard = lax.axis_index("pb") * inner_size + lax.axis_index("kv")
    own_pos = shard * shard_rows + jnp.arange(shard_rows, dtype=jnp.int32)
    initial = (start_state(teacher_q, TD, groups), start_state(student_q, SD, groups))
    key_teacher = lax.all_gather(teacher_k, ("pb", "kv"), axis=0, tiled=True)
    value_teacher = lax.all_gather(teacher_v, ("pb", "kv"), axis=0, tiled=True)
    key_student = lax.all_gather(student_k, ("pb", "kv"), axis=0, tiled=True)
    value_student = lax.all_gather(student_v, ("pb", "kv"), axis=0, tiled=True)
    piece_doc = lax.all_gather(doc_ids, ("pb", "kv"), axis=0, tiled=True)
    key_pos = jnp.arange(piece_doc.shape[0], dtype=jnp.int32)
    teacher_state = attend_keys(
        initial[0], teacher_q, own_pos, doc_ids, key_teacher, value_teacher, key_pos, piece_doc, TD
    )
    student_state = attend_keys(
        initial[1], student_q, own_pos, doc_ids, key_student, value_student, key_pos, piece_doc, SD
    )
    teacher_state, student_state = (teacher_state, student_state)
    teacher_out = finish(teacher_state[1], teacher_state[2])
    student_out = finish(student_state[1], student_state[2])
    teacher_half, student_half = (
        lax.all_to_all(teacher_out, "ha", split_axis=0, concat_axis=1, tiled=True),
        lax.all_to_all(student_out, "ha", split_axis=0, concat_axis=1, tiled=True),
    )
    count = teacher_half.shape[0]
    heads = proj_weight.shape[0]
    teacher_float = teacher_half.astype(jnp.float32)
    target = teacher_float * lax.rsqrt(
        jnp.mean(teacher_float * teacher_float, axis=1, keepdims=True) + EPSILON
    )
    student_float = student_half.astype(jnp.float32)
    features = (
        student_float
        * lax.rsqrt(jnp.mean(student_float * student_float, axis=1, keepdims=True) + EPSILON)
    ).astype(jnp.bfloat16)
    feature_heads = features.reshape(count, heads, -1)
    predicted = jnp.einsum(
        "thd,hde->the", feature_heads, proj_weight, preferred_element_type=jnp.float32
    )
    difference = predicted.reshape(count, -1) - target
    token_loss = jnp.mean(difference * difference, axis=1)
    gradient = jnp.einsum(
        "thd,the->hde",
        feature_heads.astype(jnp.float32),
        difference.reshape(count, heads, -1),
        precision=lax.Precision.HIGHEST,
    )
    gradient = (gradient / math.sqrt(total_tokens)).reshape(-1, gradient.shape[2])
    grad_w = lax.psum_scatter(gradient, ("pb", "kv", "ha"), scatter_dimension=0, tiled=True)
    return (grad_w, token_loss)


def solution(mesh):
    in_specs = (
        P(("pb", "kv"), "ha"),
        P(("pb", "kv"), "ha"),
        P(("pb", "kv"), "ha"),
        P(("pb", "kv"), "ha"),
        P(("pb", "kv"), "ha"),
        P(("pb", "kv"), "ha"),
        P(("pb", "kv")),
        P(),
    )
    out_specs = (P(("pb", "kv", "ha"), None), P(("pb", "kv", "ha")))
    return jax.shard_map(local, mesh=mesh, in_specs=in_specs, out_specs=out_specs, check_vma=False)
```

profile of v0, /device:TPU:1, one launch (start us, length us, event | category | flops | bytes accessed | tf_op | source)
XLA Modules:
  0.0 434.5 jit_solution(12670426745227966473)
XLA Ops:
  7.2 0.7 all-gather.6.cloned.1.call-update
  8.0 0.7 all-gather.8.cloned.1.call-update
  8.7 0.7 all-gather.10.cloned.1.call-update
  9.5 0.5 all-gather.12.cloned.1.call-update
  10.0 0.6 add_reduce_fusion
  10.6 34.5 %all-gather = s32[16,1,128]{2,1,0:T(1,128)S(1)} all-gather(s32[1,1,128]{2,1,0:T(1,128)} %bitcast.129), channel_id=1, replica_groups=mesh['pb'=4,'kv'=4,'ha'=2] {'pb','kv'}, dimensions={0}, use_global_device_ids=true | all-gather | bytes 8704 | tf_op jit(solution)/shard_map/all_gather | solution.py:104
  45.2 0.5 broadcast.94
  45.7 0.7 reduce.8
  46.4 1.1 copy.51
  47.5 1.3 copy.57
  48.8 0.3 copy.59
  49.1 17.9 %all-gather.6.cloned.1.call-done = bf16[2048,256]{1,0:T(8,128)(2,1)} async-done(((bf16[128,256]{1,0:T(8,128)(2,1)}), bf16[2048,256]{1,0:T(8,128)(2,1)}) %all-gather.6.cloned.1.call-update) | async-done | bytes 1048592 | tf_op jit(solution)/shard_map/all_gather | solution.py:102
  67.0 1.5 copy.52
  68.5 55.4 %all-gather.8.cloned.1.call-done = bf16[2048,256]{1,0:T(8,128)(2,1)} async-done(((bf16[128,256]{1,0:T(8,128)(2,1)}), bf16[2048,256]{1,0:T(8,128)(2,1)}) %all-gather.8.cloned.1.call-update) | async-done | bytes 1048592 | tf_op jit(solution)/shard_map/all_gather | solution.py:103
  123.9 1.5 copy.53
  125.4 0.9 broadcast_in_dim.56
  126.3 11.6 %while.30 = (s32[]{:T(128)}, f32[4,4,128]{2,1,0:T(4,128)S(1)}, f32[4,4,128]{2,1,0:T(4,128)S(1)}, f32[4,4,128,64]{2,3,1,0:T(8,128)}, s32[4,512]{1,0:T(4,128)S(1)}...) while((s32[]{:T(128)}, f32[4,4,128]{2,1,0:T(4,128)S(1)}, ...), condition=%wide.region_6.7_spmd.clone, body=%wide.region_1.6_spmd.clone.sunk | while | flops 282529920 | bytes 20069240 | solution.py:81
  126.3 0.6 constant_dynamic-slice_fusion.14
  128.1 4.1 conditional.6
  128.2 0.2 compare_and_fusion
  128.4 0.8 fusion.4
  129.2 1.0 fusion.6
  130.3 1.2 fusion.10
  131.5 0.8 copy-done.5
  132.2 0.6 constant_dynamic-slice_fusion.14
  134.1 0.6 constant_dynamic-slice_fusion.14
  136.0 0.6 constant_dynamic-slice_fusion.14
  137.9 1.1 fusion.32
  139.0 0.2 reshape.160
  139.2 0.4 copy.75
  139.6 5.6 %all_to_all.20 = bf16[2,64,1024]{2,1,0:T(8,128)(2,1)S(1)} all-to-all(bf16[2,64,1024]{2,1,0:T(8,128)(2,1)S(1)} %copy.75), channel_id=1, replica_groups=mesh['pb'=4,'kv'=4,'ha'=2] {'ha'}, dimensions={0} | all-to-all | bytes 524288 | tf_op jit(solution)/shard_map/all_to_all | solution.py:117
  145.3 0.4 copy.55
  145.7 0.6 reshape.151
  146.3 0.2 fusion.30
  146.4 0.2 multiply_convert_fusion
  146.6 1.4 copy.64
  148.0 39.2 %all-gather.10.cloned.1.call-done = bf16[2048,512]{1,0:T(8,128)(2,1)} async-done(((bf16[128,512]{1,0:T(8,128)(2,1)}), bf16[2048,512]{1,0:T(8,128)(2,1)}) %all-gather.10.cloned.1.call-update) | async-done | bytes 2097168 | tf_op jit(solution)/shard_map/all_gather | solution.py:100
  187.2 2.8 copy.58
  190.0 59.3 %all-gather.12.cloned.1.call-done = bf16[2048,512]{1,0:T(8,128)(2,1)} async-done(((bf16[128,512]{1,0:T(8,128)(2,1)}), bf16[2048,512]{1,0:T(8,128)(2,1)}) %all-gather.12.cloned.1.call-update) | async-done | bytes 2097168 | tf_op jit(solution)/shard_map/all_gather | solution.py:101
  249.3 4.1 copy.60
  253.4 1.1 broadcast_in_dim.57
  254.5 13.0 %while.31 = (s32[]{:T(128)}, f32[4,4,128]{2,1,0:T(4,128)S(1)}, f32[4,4,128]{2,1,0:T(4,128)S(1)}, f32[4,4,128,128]{3,2,1,0:T(8,128)}, s32[4,512]{1,0:T(4,128)S(1)...) while((s32[]{:T(128)}, f32[4,4,128]{2,1,0:T(4,128)S(1)}, ...), condition=%wide.region_13.14_spmd.clone, body=%wide.region_8.13_spmd.clone.sunk | while | flops 551227520 | bytes 27147128 | solution.py:81
  254.5 0.5 constant_dynamic-slice_fusion.16
  256.2 6.0 %conditional.7 = ((f32[4,4,128]{2,1,0:T(4,128)S(1)}, f32[4,4,128]{2,1,0:T(4,128)S(1)}, f32[4,4,128,128]{3,2,1,0:T(8,128)})) conditional(s32[]{:T(128)} %convert_element_type.117, (f32[4,4,128]{2,1,0:T(4,128)S(1)}, f32[4,4,128]{2,1,0:T(4,128)S(1)}, f32[4,4,128,128]{3,2,1,0:T(8,128)}) %tuple.88, (s32[128]{0:T(128)S(1)}, s32[4,512]{1,0:T(4,128)S(1)}, ...), branch_computations={%region_9.9_spmd, %region_10.12_spmd} | conditional | flops 551227520 | bytes 27142244 | solution.py:67
  256.3 0.2 compare_and_fusion.1
  256.5 1.1 constant_dynamic-slice_fusion.3
  257.6 0.9 fusion.16
  258.5 1.0 fusion.18
  259.5 1.7 fusion.22
  261.2 1.0 copy-done.3
  262.2 0.5 constant_dynamic-slice_fusion.16
  264.0 0.5 constant_dynamic-slice_fusion.16
  265.8 0.5 constant_dynamic-slice_fusion.16
  267.5 1.6 fusion.31
  269.1 0.4 copy.61
  269.5 0.4 convert_element_type.80
  269.9 4.9 %all_to_all.21 = bf16[2,64,2048]{2,1,0:T(8,128)(2,1)S(1)} all-to-all(bf16[2,64,2048]{2,1,0:T(8,128)(2,1)S(1)} %convert_element_type.80), channel_id=1, replica_groups=mesh['pb'=4,'kv'=4,'ha'=2] {'ha'}, dimensions={0} | all-to-all | bytes 1048576 | tf_op jit(solution)/shard_map/all_to_all | solution.py:116
  274.9 1.8 copy.62
  276.7 2.1 reshape.152
  278.8 0.2 fusion.29
  279.0 0.9 multiply_reduce_fusion
  280.0 1.6 convolution_multiply_fusion
  281.6 0.5 broadcast_multiply_fusion
  282.1 145.9 %reduce-scatter.2.cloned.1.call-done = f32[64,128]{1,0:T(8,128)} async-done(((f32[2048,128]{1,0:T(8,128)}), f32[64,128]{1,0:T(8,128)}) %reduce-scatter.2.cloned.1.call-update) | async-done | bytes 32784 | tf_op jit(solution)/shard_map/reduce_scatter | solution.py:143
  (61 shorter events, 0.7 us)
Async XLA Ops:
  7.2 271.9 %copy-start = (bf16[32,64,128]{2,1,0:T(8,128)(2,1)S(1)}, bf16[32,64,128]{2,1,0:T(8,128)(2,1)}, u32[]{:S(2)}) copy-start(bf16[32,64,128]{2,1,0:T(8,128)(2,1)} %param.23) | copy-start | bytes 1572868
  7.2 119.1 %copy-start.6 = (s32[128]{0:T(128)S(1)}, s32[128]{0:T(128)}, u32[]{:S(2)}) copy-start(s32[128]{0:T(128)} %param.22) | copy-start | bytes 1540
  7.2 59.8 %all-gather.6.cloned.1.call-start = ((), (), s32[]{:S(2)}) async-start(), calls=%async_computation.3 | async-start | bytes 1114112 | tf_op jit(solution)/shard_map/all_gather | solution.py:102
  7.9 116.0 %all-gather.8.cloned.1.call-start = ((), (), s32[]{:S(2)}) async-start(), calls=%async_computation.4 | async-start | bytes 1114112 | tf_op jit(solution)/shard_map/all_gather | solution.py:103
  8.7 178.5 %all-gather.10.cloned.1.call-start = ((), (), s32[]{:S(2)}) async-start(), calls=%async_computation.5 | async-start | bytes 2228224 | tf_op jit(solution)/shard_map/all_gather | solution.py:100
  9.4 239.9 %all-gather.12.cloned.1.call-start = ((), (), s32[]{:S(2)}) async-start(), calls=%async_computation.6 | async-start | bytes 2228224 | tf_op jit(solution)/shard_map/all_gather | solution.py:101
  10.0 418.0 %reduce-scatter.2.cloned.1.call-start = ((), (), s32[]{:S(2)}) async-start(), calls=%async_computation.7 | async-start | bytes 1081344 | tf_op jit(solution)/shard_map/reduce_scatter | solution.py:143
  128.4 1.8 copy-start.4
  131.4 0.8 copy-start.5
  257.6 1.9 copy-start.2
  261.2 1.0 copy-start.3
  269.5 9.5 %copy-start.1 = (bf16[64,32,64]{0,2,1:T(8,128)(2,1)S(1)}, bf16[64,32,64]{0,2,1:T(8,128)(2,1)}, u32[]{:S(2)}) copy-start(bf16[64,32,64]{0,2,1:T(8,128)(2,1)} %copy.64) | copy-start | bytes 786436
Sparse Core Ops, SparseCore 0:
  10.8 56.1 all-gather.5
  69.7 54.1 all-gather.7
  126.7 60.4 all-gather.9
  189.9 59.3 all-gather.11
  281.7 146.2 reduce-scatter.1
where the time goes:
time: 441 us; the launch traced here: 435 us
  waiting for transfers between devices  320 us (73%)
  blocking collectives  45 us (10%)
  local copies, waits for them, and re-layouts  30.2 us (7%)
  between operations  14 us (3%)
  loops' own time  10.2 us (2%)
  other arithmetic  7.57 us (2%)
  matrix products  7.04 us (2%)
    reduce_scatter x1, waiting for transfers between devices, local(): lax.psum_scatter(gradient, ('pb', 'kv', 'ha'), scatter_dimension=0, tiled...  146 us
    all_gather x1, waiting for transfers between devices, local(): value_teacher = lax.all_gather(teacher_v, ('pb', 'kv'), axis=0, tiled=True)  59.3 us
    all_gather x1, waiting for transfers between devices, local(): value_student = lax.all_gather(student_v, ('pb', 'kv'), axis=0, tiled=True)  55.4 us
    all_gather x1, waiting for transfers between devices, local(): key_teacher = lax.all_gather(teacher_k, ('pb', 'kv'), axis=0, tiled=True)  39.2 us
    all_gather x1, blocking collectives, local(): piece_doc = lax.all_gather(doc_ids, ('pb', 'kv'), axis=0, tiled=True)  34.5 us
    all_gather x1, waiting for transfers between devices, local(): key_student = lax.all_gather(student_k, ('pb', 'kv'), axis=0, tiled=True)  17.9 us
    unnamed x13, local copies, waits for them, and re-layouts  12.6 us
    another operation x2, loops' own time, attend_keys(): final, unused = lax.scan(visit, state, items)  9.97 us
  transfers between devices with their start and end apart: 5, of which 5 were waited for; matrix products, arithmetic and copies ran while one was open for 5% of the time, Pallas kernels for 0%

commit v1 on v0

--- a/solution.py
+++ b/solution.py
@@ -1,12 +1,18 @@
+import functools
 import math
 
 import jax
 import jax.numpy as jnp
 from jax import lax
+from jax.experimental import pallas as pl
+from jax.experimental.pallas import tpu as pltpu
 from jax.sharding import PartitionSpec as P
+
+MESH = pl.DeviceIdType.MESH
 
 TD = 128
 SD = 64
+DOCS = 4
 
 
 NEGATIVE = -1e30
@@ -88,7 +94,7 @@
     return jnp.transpose(result, (2, 0, 1, 3)).reshape(queried, -1).astype(jnp.bfloat16)
 
 
-def local(teacher_q, teacher_k, teacher_v, student_q, student_k, student_v, doc_ids, proj_weight):
+def gathered(teacher_q, teacher_k, teacher_v, student_q, student_k, student_v, doc_ids, proj_weight):
     shard_rows = teacher_q.shape[0]
     groups = teacher_k.shape[1] // TD
     outer = lax.axis_size("pb")
@@ -143,6 +149,495 @@
     grad_w = lax.psum_scatter(gradient, ("pb", "kv", "ha"), scatter_dimension=0, tiled=True)
     return (grad_w, token_loss)
 
+def rows_dot(a, b):
+    return lax.dot_general(a, b, (((1,), (1,)), ((), ())), preferred_element_type=jnp.float32)
+
+
+def columns_dot(a, b):
+    return lax.dot_general(a, b, (((0,), (0,)), ((), ())), preferred_element_type=jnp.float32)
+
+
+def fused(
+    shape,
+    tokens,
+    tq_ref,
+    tk_ref,
+    tv_ref,
+    sq_ref,
+    sk_ref,
+    sv_ref,
+    doc_ref,
+    w_ref,
+    grad_ref,
+    loss_ref,
+    stage,
+    kv,
+    tq_in,
+    sq_in,
+    tq_all,
+    sq_all,
+    t_acc,
+    s_acc,
+    soft,
+    stats,
+    losses,
+    grads,
+    grads_in,
+    xy_send,
+    xy_recv,
+    q_send,
+    q_recv,
+    up_send,
+    up_recv,
+    down_send,
+    down_recv,
+    stat_send,
+    stat_recv,
+    loss_send,
+    loss_recv,
+    grad_send,
+    grad_recv,
+):
+    npb, nkv, nha = shape
+    devices = npb * nkv * nha
+    rows = tq_ref.shape[0]
+    heads = tq_ref.shape[1] // (npb * TD)
+    wide = heads * rows
+    pb, z, ha = lax.axis_index("pb"), lax.axis_index("kv"), lax.axis_index("ha")
+    me = (pb * nkv + z) * nha + ha
+
+    def coords(index):
+        return (index // (nkv * nha), (index // nha) % nkv, index % nha)
+
+    barrier = pltpu.get_barrier_semaphore()
+
+    def greet(r, carry):
+        pl.semaphore_signal(
+            barrier, inc=1, device_id=coords((me + r) % devices), device_id_type=MESH
+        )
+        return carry
+
+    lax.fori_loop(1, devices, greet, 0)
+
+    doc_rows = jnp.broadcast_to(doc_ref[...].astype(jnp.float32), (16, rows)).astype(jnp.bfloat16)
+    for g in range(npb):
+        stage[g, 0:rows, :] = tk_ref[:, g * TD : (g + 1) * TD]
+        stage[g, rows : 2 * rows, :] = tv_ref[:, g * TD : (g + 1) * TD]
+        stage[g, 2 * rows : 3 * rows, :] = jnp.concatenate(
+            [sk_ref[:, g * SD : (g + 1) * SD], sv_ref[:, g * SD : (g + 1) * SD]], axis=1
+        )
+        stage[g, 3 * rows : 3 * rows + 16, :] = doc_rows
+    kv[z, pb] = stage[pb]
+
+    pl.semaphore_wait(barrier, devices - 1)
+
+    def partner(r):
+        return ((pb // 2 + r // 2) % 2) * 2 + (pb % 2 + r % 2) % 2
+
+    def kv_copy(r):
+        to = partner(r)
+        return pltpu.make_async_remote_copy(
+            src_ref=stage.at[to],
+            dst_ref=kv.at[z, pb],
+            send_sem=xy_send.at[r],
+            recv_sem=xy_recv.at[r],
+            device_id=(to, z, ha),
+            device_id_type=MESH,
+        )
+
+    def q_copy(r, which):
+        to = partner(r)
+        ref, into, width = ((tq_ref, tq_in, heads * TD), (sq_ref, sq_in, heads * SD))[which]
+        return pltpu.make_async_remote_copy(
+            src_ref=ref.at[:, pl.ds(pl.multiple_of(to * width, width), width)],
+            dst_ref=into.at[pb],
+            send_sem=q_send.at[r, which],
+            recv_sem=q_recv.at[r, which],
+            device_id=(to, z, ha),
+            device_id_type=MESH,
+        )
+
+    for r in range(1, npb):
+        kv_copy(r).start()
+    for r in range(1, npb):
+        q_copy(r, 0).start()
+        q_copy(r, 1).start()
+
+    def chain(h, r, up):
+        source = z - h if up else z + h
+        piece = kv.at[source, partner(r)]
+        send, recv = (up_send, up_recv) if up else (down_send, down_recv)
+        return pltpu.make_async_remote_copy(
+            src_ref=piece,
+            dst_ref=piece,
+            send_sem=send.at[h, r],
+            recv_sem=recv.at[h, r],
+            device_id=(pb, z + 1 if up else z - 1, ha),
+            device_id_type=MESH,
+        )
+
+    def arrived(h, r, up):
+        source = z - h if up else z + h
+        piece = kv.at[source, partner(r)]
+        recv = up_recv if up else down_recv
+        send = up_send if up else down_send
+        pltpu.make_async_remote_copy(
+            src_ref=piece,
+            dst_ref=piece,
+            send_sem=send.at[h - 1, r],
+            recv_sem=recv.at[h - 1, r],
+            device_id=(pb, z - 1 if up else z + 1, ha),
+            device_id_type=MESH,
+        ).wait_recv()
+
+    def first_hop():
+        for r in range(npb):
+            if r > 0:
+                kv_copy(r).wait_recv()
+
+            @pl.when(z < nkv - 1)
+            def _():
+                chain(0, r, True).start()
+
+            @pl.when(z > 0)
+            def _():
+                chain(0, r, False).start()
+
+    def next_hop(h):
+        for r in range(npb):
+
+            @pl.when(z - h >= 0)
+            def _():
+                arrived(h, r, True)
+
+                @pl.when(z < nkv - 1)
+                def _():
+                    chain(h, r, True).start()
+
+            @pl.when(z + h <= nkv - 1)
+            def _():
+                arrived(h, r, False)
+
+                @pl.when(z > 0)
+                def _():
+                    chain(h, r, False).start()
+
+    first_hop()
+    next_hop(1)
+
+    tq_in[pb] = tq_ref[:, pl.ds(pl.multiple_of(pb * heads * TD, heads * TD), heads * TD)]
+    sq_in[pb] = sq_ref[:, pl.ds(pl.multiple_of(pb * heads * SD, heads * SD), heads * SD)]
+    for r in range(1, npb):
+        q_copy(r, 0).wait_recv()
+        q_copy(r, 1).wait_recv()
+    blank = jnp.zeros((rows, TD - SD), jnp.bfloat16)
+    for p in range(npb):
+        for j in range(heads):
+            tq_all[p, j * rows : (j + 1) * rows, :] = tq_in[p, :, j * TD : (j + 1) * TD]
+            sq_all[p, j * rows : (j + 1) * rows, :] = jnp.concatenate(
+                [sq_in[p, :, j * SD : (j + 1) * SD], blank], axis=1
+            )
+    t_acc[...] = jnp.zeros_like(t_acc)
+    s_acc[...] = jnp.zeros_like(s_acc)
+    soft[:, 0:2, :] = jnp.full((npb, 2, wide), NEGATIVE, jnp.float32)
+    soft[:, 2:4, :] = jnp.zeros((npb, 2, wide), jnp.float32)
+
+    local_key = lax.broadcasted_iota(jnp.int32, (rows, wide), 0)
+    local_query = lax.broadcasted_iota(jnp.int32, (1, wide), 1) % rows
+
+    def attend(source):
+        firsts = []
+        for c in range(npb):
+            key_doc = kv[source, c, 3 * rows : 3 * rows + 16, :].astype(jnp.float32)[0:1, :]
+            firsts.append(
+                [
+                    jnp.sum((key_doc < d).astype(jnp.float32), axis=1, keepdims=True)
+                    for d in range(1, DOCS)
+                ]
+            )
+        for p in range(npb):
+            keys = (p + 1) * rows
+            own = kv[z, p, 3 * rows : 3 * rows + 16, :].astype(jnp.float32)[0:1, :]
+            query_doc = jnp.concatenate([own] * heads, axis=1)
+            allowed = []
+            for c in range(p + 1):
+                least = jnp.zeros((1, wide), jnp.float32)
+                for d in range(1, DOCS):
+                    least = jnp.where(query_doc == d, firsts[c][d - 1], least)
+                ok = local_key >= least.astype(jnp.int32)
+                if c == p:
+                    ok = ok & (local_key <= local_query + (z - source) * rows)
+                allowed.append(ok)
+            for which in range(2):
+                size = (TD, SD)[which]
+                factor = math.log2(math.e) / math.sqrt(size)
+                queries = (tq_all, sq_all)[which][p]
+                if which == 0:
+                    key_rows = kv[source, 0 : p + 1, 0:rows, :].reshape(keys, TD)
+                    value_rows = kv[source, 0 : p + 1, rows : 2 * rows, :].reshape(keys, TD)
+                else:
+                    key_rows = kv[source, 0 : p + 1, 2 * rows : 3 * rows, :].reshape(keys, TD)
+                    value_rows = key_rows
+                raw = rows_dot(key_rows, queries) * factor
+                scores = jnp.concatenate(
+                    [
+                        jnp.where(allowed[c], raw[c * rows : (c + 1) * rows], NEGATIVE)
+                        for c in range(p + 1)
+                    ],
+                    axis=0,
+                )
+                old = soft[p, which : which + 1, :]
+                new = jnp.maximum(old, jnp.max(scores, axis=0, keepdims=True))
+                weights = jnp.exp2(scores - new)
+                shrink = jnp.exp2(old - new)
+                soft[p, which : which + 1, :] = new
+                soft[p, which + 2 : which + 3, :] = soft[
+                    p, which + 2 : which + 3, :
+                ] * shrink + jnp.sum(weights, axis=0, keepdims=True)
+                mixed = columns_dot(value_rows, weights.astype(jnp.bfloat16))
+                if which == 0:
+                    t_acc[p] = t_acc[p] * shrink + mixed
+                else:
+                    s_acc[p] = s_acc[p] * shrink + mixed[TD - SD :]
+
+    def turn(h, carry):
+        @pl.when(h >= 2)
+        def _():
+            next_hop(h)
+
+        below = (z - h >= 0).astype(jnp.int32)
+        above = ((z + h <= nkv - 1) & (h > 0)).astype(jnp.int32)
+
+        def visit(i, inner):
+            attend(jnp.where((i == 0) & (below == 1), z - h, z + h))
+            return inner
+
+        lax.fori_loop(0, below + above, visit, 0)
+        return carry
+
+    lax.fori_loop(0, nkv, turn, 0)
+
+    def by_token(row):
+        total = row[:, 0:rows]
+        for j in range(1, heads):
+            total = total + row[:, j * rows : (j + 1) * rows]
+        return total
+
+    t_sums, s_sums, t_outs, s_outs = [], [], [], []
+    for p in range(npb):
+        t_out = (t_acc[p] / soft[p, 2:3, :]).astype(jnp.bfloat16).astype(jnp.float32)
+        s_out = (s_acc[p] / soft[p, 3:4, :]).astype(jnp.bfloat16).astype(jnp.float32)
+        t_acc[p] = t_out
+        s_acc[p] = s_out
+        t_sums.append(by_token(jnp.sum(t_out * t_out, axis=0, keepdims=True)))
+        s_sums.append(by_token(jnp.sum(s_out * s_out, axis=0, keepdims=True)))
+
+    plane = npb * nha
+    slot = pb * nha + ha
+
+    def share(buffer, send, recv, r):
+        to = (slot + r) % plane
+        return pltpu.make_async_remote_copy(
+            src_ref=buffer.at[slot],
+            dst_ref=buffer.at[slot],
+            send_sem=send.at[r],
+            recv_sem=recv.at[r],
+            device_id=(to // nha, z, to % nha),
+            device_id_type=MESH,
+        )
+
+    stats[slot] = jnp.concatenate(t_sums + s_sums, axis=0)
+    for r in range(1, plane):
+        share(stats, stat_send, stat_recv, r).start()
+    for r in range(1, plane):
+        share(stats, stat_send, stat_recv, r).wait_recv()
+    sums = stats[0]
+    for i in range(1, plane):
+        sums = sums + stats[i]
+    t_scale = lax.rsqrt(sums[0:npb] * (1.0 / (heads * plane * TD)) + EPSILON)
+    s_scale = lax.rsqrt(sums[npb : 2 * npb] * (1.0 / (heads * plane * SD)) + EPSILON)
+
+    loss = jnp.zeros((1, npb * rows), jnp.float32)
+    first_head = (ha * npb + pb) * heads
+    features, differences = [], []
+    for j in range(heads):
+        cut = slice(j * rows, (j + 1) * rows)
+        target = jnp.concatenate(
+            [t_acc[p, :, cut] * t_scale[p : p + 1] for p in range(npb)], axis=1
+        )
+        feature = jnp.concatenate(
+            [s_acc[p, :, cut] * s_scale[p : p + 1] for p in range(npb)], axis=1
+        ).astype(jnp.bfloat16)
+        difference = columns_dot(w_ref[first_head + j], feature) - target
+        loss = loss + jnp.sum(difference * difference, axis=0, keepdims=True)
+        features.append(feature)
+        differences.append(difference)
+    losses[slot] = jnp.concatenate(
+        [loss[:, p * rows : (p + 1) * rows] for p in range(npb)]
+        + [jnp.zeros((8 - npb, rows), jnp.float32)],
+        axis=0,
+    )
+    for r in range(1, plane):
+        share(losses, loss_send, loss_recv, r).start()
+
+    def grad_copy(j):
+        return pltpu.make_async_remote_copy(
+            src_ref=grads.at[j],
+            dst_ref=grads_in.at[z],
+            send_sem=grad_send.at[j],
+            recv_sem=grad_recv.at[z],
+            device_id=coords(first_head + j),
+            device_id_type=MESH,
+        )
+
+    for j in range(heads):
+        high = differences[j].astype(jnp.bfloat16)
+        low = (differences[j] - high.astype(jnp.float32)).astype(jnp.bfloat16)
+        grads[j] = rows_dot(features[j], high) + rows_dot(features[j], low)
+
+        @pl.when(first_head + j != me)
+        def _():
+            grad_copy(j).start()
+
+        @pl.when(first_head + j == me)
+        def _():
+            grads_in[z] = grads[j]
+
+    for r in range(1, plane):
+        share(losses, loss_send, loss_recv, r).wait_recv()
+    mine = losses[0, pl.ds(pb, 1), :]
+    for i in range(1, plane):
+        mine = mine + losses[i, pl.ds(pb, 1), :]
+    part = rows // nha
+    chosen = mine[:, 0:part]
+    for i in range(1, nha):
+        chosen = jnp.where(ha == i, mine[:, i * part : (i + 1) * part], chosen)
+    loss_ref[...] = chosen * (1.0 / (heads * plane * TD))
+
+    giver_ha = me // (npb * heads)
+    giver_pb = (me // heads) % npb
+    for i in range(nkv):
+
+        @pl.when((giver_ha != ha) | (giver_pb != pb) | (z != i))
+        def _():
+            pltpu.make_async_remote_copy(
+                src_ref=grads.at[0],
+                dst_ref=grads_in.at[i],
+                send_sem=grad_send.at[0],
+                recv_sem=grad_recv.at[i],
+                device_id=(giver_pb, i, giver_ha),
+                device_id_type=MESH,
+            ).wait_recv()
+
+    total = grads_in[0]
+    for i in range(1, nkv):
+        total = total + grads_in[i]
+    grad_ref[...] = total * (1.0 / math.sqrt(tokens))
+
+    for r in range(1, npb):
+        kv_copy(r).wait_send()
+        q_copy(r, 0).wait_send()
+        q_copy(r, 1).wait_send()
+    for h in range(nkv - 1):
+        for r in range(npb):
+
+            @pl.when((z - h >= 0) & (z < nkv - 1))
+            def _():
+                chain(h, r, True).wait_send()
+
+            @pl.when((z + h <= nkv - 1) & (z > 0))
+            def _():
+                chain(h, r, False).wait_send()
+
+    for r in range(1, plane):
+        share(stats, stat_send, stat_recv, r).wait_send()
+        share(losses, loss_send, loss_recv, r).wait_send()
+    for j in range(heads):
+
+        @pl.when(first_head + j != me)
+        def _():
+            grad_copy(j).wait_send()
+
+
+def by_heads(
+    shape, teacher_q, teacher_k, teacher_v, student_q, student_k, student_v, doc_ids, proj_weight
+):
+    npb, nkv, nha = shape
+    rows = teacher_q.shape[0]
+    heads = teacher_q.shape[1] // (npb * TD)
+    wide = heads * rows
+    plane = npb * nha
+    dma = pltpu.SemaphoreType.DMA
+    bf16, f32 = jnp.bfloat16, jnp.float32
+    vmem = pl.BlockSpec(memory_space=pltpu.VMEM)
+    grad, loss = pl.pallas_call(
+        functools.partial(fused, shape, rows * npb * nkv),
+        out_shape=(
+            jax.ShapeDtypeStruct((SD, TD), f32),
+            jax.ShapeDtypeStruct((1, rows // nha), f32),
+        ),
+        in_specs=[vmem] * 8,
+        out_specs=(vmem, vmem),
+        scratch_shapes=[
+            pltpu.VMEM((npb, 3 * rows + 16, TD), bf16),
+            pltpu.VMEM((nkv, npb, 3 * rows + 16, TD), bf16),
+            pltpu.VMEM((npb, rows, heads * TD), bf16),
+            pltpu.VMEM((npb, rows, heads * SD), bf16),
+            pltpu.VMEM((npb, wide, TD), bf16),
+            pltpu.VMEM((npb, wide, TD), bf16),
+            pltpu.VMEM((npb, TD, wide), f32),
+            pltpu.VMEM((npb, SD, wide), f32),
+            pltpu.VMEM((npb, 8, wide), f32),
+            pltpu.VMEM((plane, 8, rows), f32),
+            pltpu.VMEM((plane, 8, rows), f32),
+            pltpu.VMEM((heads, SD, TD), f32),
+            pltpu.VMEM((nkv, SD, TD), f32),
+            dma((npb,)),
+            dma((npb,)),
+            dma((npb, 2)),
+            dma((npb, 2)),
+            dma((nkv, npb)),
+            dma((nkv, npb)),
+            dma((nkv, npb)),
+            dma((nkv, npb)),
+            dma((plane,)),
+            dma((plane,)),
+            dma((plane,)),
+            dma((plane,)),
+            dma((heads,)),
+            dma((nkv,)),
+        ],
+        compiler_params=pltpu.CompilerParams(
+            collective_id=0, has_side_effects=True, vmem_limit_bytes=48 * 1024 * 1024
+        ),
+        name="attention_distillation",
+    )(
+        teacher_q,
+        teacher_k,
+        teacher_v,
+        student_q,
+        student_k,
+        student_v,
+        doc_ids.reshape(1, rows),
+        proj_weight,
+    )
+    return grad, loss.reshape(-1)
+
+
+def local(*arguments):
+    teacher_q, teacher_k, proj_weight = arguments[0], arguments[1], arguments[7]
+    shape = tuple(lax.axis_size(name) for name in ("pb", "kv", "ha"))
+    groups = teacher_k.shape[1] // TD
+    fits = (
+        groups == shape[0] == 4
+        and shape[2] == 2
+        and math.prod(shape) == proj_weight.shape[0]
+        and teacher_q.shape[0] == 128
+    )
+    if fits:
+        return by_heads(shape, *arguments)
+    return gathered(*arguments)
+
 
 def solution(mesh):
     in_specs = (

time: 441 us -> 64.9 us (0.15); the launches traced: 435 us -> 64.2 us
  waiting for transfers between devices: 320 us -> 0 us
  Pallas kernels: 0 us -> 55.3 us
  blocking collectives: 45 us -> 0 us
  local copies, waits for them, and re-layouts: 30.2 us -> 8.29 us
  between operations: 14 us -> 0.66 us
  loops' own time: 10.2 us -> 0 us
  other arithmetic: 7.57 us -> 0 us
  matrix products: 7.04 us -> 0 us
    all_gather x4 -> x0, waiting for transfers between devices: 172 us -> none  [the longest x1 59.3 us: local(): value_teacher = lax.all_gather(teacher_v, ('pb', 'kv'), axis=0, tiled=True)]
    reduce_scatter x1 -> x0, waiting for transfers between devices: 146 us -> none  [local(): lax.psum_scatter(gradient, ('pb', 'kv', 'ha'), scatter_dimension=0, tiled...]
    pallas_call x0 -> x1, Pallas kernels: none -> 55.3 us  [by_heads(): pl.pallas_call(functools.partial(fused, shape, rows * npb * nkv), out_sha...]
    all_gather x1 -> x0, blocking collectives: 34.5 us -> none  [local(): piece_doc = lax.all_gather(doc_ids, ('pb', 'kv'), axis=0, tiled=True)]
    all_to_all x2 -> x0, blocking collectives: 10.5 us -> none  [the longest x1 5.6 us: local(): lax.all_to_all(student_out, 'ha', split_axis=0, concat_axis=1, tiled=True)]
    another operation x10 -> x0, loops' own time: 10.2 us -> none  [the longest x2 9.97 us: attend_keys(): final, unused = lax.scan(visit, state, items)]
    convert_element_type x9 -> x0, local copies, waits for them, and re-layouts: 7.65 us -> none  [the longest x2 3.84 us: local(): teacher_float = teacher_half.astype(jnp.float32)]
    dot_general x6 -> x0, matrix products: 7.04 us -> none  [the longest x2 2.85 us: compute(): jnp.einsum('gpqk,kgd->gpqd', weights.astype(jnp.bfloat16), value_block.re...]
  transfers between devices with their start and end apart: 5 -> 0, of which waited for: 5 -> 0; matrix products, arithmetic and copies ran while one was open for 5% -> 0% of each run, Pallas kernels for 0% -> 0%
where the time goes in v1:
time: 64.9 us; the launch traced here: 64.2 us
  Pallas kernels  55.3 us (85%)
  local copies, waits for them, and re-layouts  8.29 us (13%)
  between operations  0.66 us (1%)
    pallas_call x1, Pallas kernels, by_heads(): pl.pallas_call(functools.partial(fused, shape, rows * npb * nkv), out_sha...  55.3 us
    unnamed x18, local copies, waits for them, and re-layouts  8.29 us

profile of v1, /device:TPU:1, one launch (start us, length us, event | category | flops | bytes accessed | tf_op | source)
XLA Modules:
  0.0 64.2 jit_solution(5515981473606892186)
XLA Ops:
  0.6 0.0 copy-start.7
  0.6 0.6 %copy-done.7 = s32[128]{0:T(128)S(1)} copy-done((s32[128]{0:T(128)S(1)}, s32[128]{0:T(128)}, u32[]{:S(2)}) %copy-start.7) | copy-done | bytes 536
  1.3 0.0 copy-start
  1.3 1.0 %copy-done = bf16[128,2048]{1,0:T(8,128)(2,1)S(1)} copy-done((bf16[128,2048]{1,0:T(8,128)(2,1)S(1)}, bf16[128,2048]{1,0:T(8,128)(2,1)}, u32[]{:S(2)}) %copy-start) | copy-done | bytes 524312
  2.3 0.0 copy-start.1
  2.3 1.0 %copy-done.1 = bf16[32,64,128]{2,1,0:T(8,128)(2,1)S(1)} copy-done((bf16[32,64,128]{2,1,0:T(8,128)(2,1)S(1)}, bf16[32,64,128]{2,1,0:T(8,128)(2,1)}, u32[]{:S(2)}) %copy-start.1) | copy-done | bytes 524312
  3.4 0.0 copy-start.2
  3.4 0.9 %copy-done.2 = bf16[128,1024]{1,0:T(8,128)(2,1)S(1)} copy-done((bf16[128,1024]{1,0:T(8,128)(2,1)S(1)}, bf16[128,1024]{1,0:T(8,128)(2,1)}, u32[]{:S(2)}) %copy-start.2) | copy-done | bytes 262168
  4.3 0.0 copy-start.3
  4.3 0.9 %copy-done.3 = bf16[128,512]{1,0:T(8,128)(2,1)S(1)} copy-done((bf16[128,512]{1,0:T(8,128)(2,1)S(1)}, bf16[128,512]{1,0:T(8,128)(2,1)}, u32[]{:S(2)}) %copy-start.3) | copy-done | bytes 131096
  5.2 0.0 copy-start.4
  5.2 0.9 %copy-done.4 = bf16[128,512]{1,0:T(8,128)(2,1)S(1)} copy-done((bf16[128,512]{1,0:T(8,128)(2,1)S(1)}, bf16[128,512]{1,0:T(8,128)(2,1)}, u32[]{:S(2)}) %copy-start.4) | copy-done | bytes 131096
  6.1 0.0 copy-start.5
  6.1 0.8 %copy-done.5 = bf16[128,256]{1,0:T(8,128)(2,1)S(1)} copy-done((bf16[128,256]{1,0:T(8,128)(2,1)S(1)}, bf16[128,256]{1,0:T(8,128)(2,1)}, u32[]{:S(2)}) %copy-start.5) | copy-done | bytes 65560
  7.0 0.0 copy-start.6
  7.0 0.8 %copy-done.6 = bf16[128,256]{1,0:T(8,128)(2,1)S(1)} copy-done((bf16[128,256]{1,0:T(8,128)(2,1)S(1)}, bf16[128,256]{1,0:T(8,128)(2,1)}, u32[]{:S(2)}) %copy-start.6) | copy-done | bytes 65560
  7.8 55.3 %attention_distillation.1 = (f32[64,128]{1,0:T(8,128)S(1)}, f32[1,64]{1,0:T(1,128)S(1)}) custom-call(bf16[128,2048]{1,0:T(8,128)(2,1)S(1)} %copy-done, bf16[128,512]{1,0:T(8,128)(2,1)S(1)} %copy-done.3, bf16[128,512]{1,0:T(8,128)(2,1)S(1)} %copy-done.4, bf16[128,1024]{1,0:T(8,128)(2,1)S(1)} %copy-done.2, bf16[128,256]{1,0:T(8,128)(2,1)S(1)} %copy-done.5, ...), custom_call_target="tpu_custom_call" | custom-call | tf_op jit(solution)/shard_map/attention_distillation/pallas_call | solution.py:573
  63.1 0.6 copy.12
  63.7 0.5 copy.13
Async XLA Ops:
  0.6 0.7 %copy-start.7 = (s32[128]{0:T(128)S(1)}, s32[128]{0:T(128)}, u32[]{:S(2)}) copy-start(s32[128]{0:T(128)} %param.14) | copy-start | bytes 1540
  1.3 1.0 %copy-start = (bf16[128,2048]{1,0:T(8,128)(2,1)S(1)}, bf16[128,2048]{1,0:T(8,128)(2,1)}, u32[]{:S(2)}) copy-start(bf16[128,2048]{1,0:T(8,128)(2,1)} %tq_ref.1) | copy-start | bytes 1572868
  2.3 1.0 %copy-start.1 = (bf16[32,64,128]{2,1,0:T(8,128)(2,1)S(1)}, bf16[32,64,128]{2,1,0:T(8,128)(2,1)}, u32[]{:S(2)}) copy-start(bf16[32,64,128]{2,1,0:T(8,128)(2,1)} %w_ref.1) | copy-start | bytes 1572868
  3.4 0.9 %copy-start.2 = (bf16[128,1024]{1,0:T(8,128)(2,1)S(1)}, bf16[128,1024]{1,0:T(8,128)(2,1)}, u32[]{:S(2)}) copy-start(bf16[128,1024]{1,0:T(8,128)(2,1)} %sq_ref.1) | copy-start | bytes 786436
  4.3 0.9 %copy-start.3 = (bf16[128,512]{1,0:T(8,128)(2,1)S(1)}, bf16[128,512]{1,0:T(8,128)(2,1)}, u32[]{:S(2)}) copy-start(bf16[128,512]{1,0:T(8,128)(2,1)} %tk_ref.1) | copy-start | bytes 393220
  5.2 0.9 %copy-start.4 = (bf16[128,512]{1,0:T(8,128)(2,1)S(1)}, bf16[128,512]{1,0:T(8,128)(2,1)}, u32[]{:S(2)}) copy-start(bf16[128,512]{1,0:T(8,128)(2,1)} %tv_ref.1) | copy-start | bytes 393220
  6.1 0.8 %copy-start.5 = (bf16[128,256]{1,0:T(8,128)(2,1)S(1)}, bf16[128,256]{1,0:T(8,128)(2,1)}, u32[]{:S(2)}) copy-start(bf16[128,256]{1,0:T(8,128)(2,1)} %sk_ref.1) | copy-start | bytes 196612
  7.0 0.8 %copy-start.6 = (bf16[128,256]{1,0:T(8,128)(2,1)S(1)}, bf16[128,256]{1,0:T(8,128)(2,1)}, u32[]{:S(2)}) copy-start(bf16[128,256]{1,0:T(8,128)(2,1)} %sv_ref.1) | copy-start | bytes 196612

commit v2 on v1

--- a/solution.py
+++ b/solution.py
@@ -161,15 +161,21 @@
     shape,
     tokens,
     tq_ref,
+    tk_hbm,
+    tv_hbm,
+    sq_ref,
+    sk_hbm,
+    sv_hbm,
+    doc_hbm,
+    w_hbm,
+    grad_ref,
+    loss_ref,
     tk_ref,
     tv_ref,
-    sq_ref,
     sk_ref,
     sv_ref,
     doc_ref,
     w_ref,
-    grad_ref,
-    loss_ref,
     stage,
     kv,
     tq_in,
@@ -197,6 +203,7 @@
     loss_recv,
     grad_send,
     grad_recv,
+    load_sem,
 ):
     npb, nkv, nha = shape
     devices = npb * nkv * nha
@@ -209,6 +216,30 @@
     def coords(index):
         return (index // (nkv * nha), (index // nha) % nkv, index % nha)
 
+    first_head = (ha * npb + pb) * heads
+
+    def query_part(place, which):
+        ref, width = ((tq_ref, heads * TD), (sq_ref, heads * SD))[which]
+        return ref.at[:, pl.ds(pl.multiple_of(place * width, width), width)]
+
+    loads = [
+        pltpu.make_async_copy(source, into, load_sem.at[i])
+        for i, (source, into) in enumerate(
+            (
+                (tk_hbm, tk_ref),
+                (tv_hbm, tv_ref),
+                (sk_hbm, sk_ref),
+                (sv_hbm, sv_ref),
+                (doc_hbm, doc_ref),
+                (w_hbm.at[pl.ds(first_head, heads)], w_ref),
+                (query_part(pb, 0), tq_in.at[pb]),
+                (query_part(pb, 1), sq_in.at[pb]),
+            )
+        )
+    ]
+    for load in loads:
+        load.start()
+
     barrier = pltpu.get_barrier_semaphore()
 
     def greet(r, carry):
@@ -219,6 +250,8 @@
 
     lax.fori_loop(1, devices, greet, 0)
 
+    for load in loads[:5]:
+        load.wait()
     doc_rows = jnp.broadcast_to(doc_ref[...].astype(jnp.float32), (16, rows)).astype(jnp.bfloat16)
     for g in range(npb):
         stage[g, 0:rows, :] = tk_ref[:, g * TD : (g + 1) * TD]
@@ -247,10 +280,9 @@
 
     def q_copy(r, which):
         to = partner(r)
-        ref, into, width = ((tq_ref, tq_in, heads * TD), (sq_ref, sq_in, heads * SD))[which]
         return pltpu.make_async_remote_copy(
-            src_ref=ref.at[:, pl.ds(pl.multiple_of(to * width, width), width)],
-            dst_ref=into.at[pb],
+            src_ref=query_part(to, which),
+            dst_ref=(tq_in, sq_in)[which].at[pb],
             send_sem=q_send.at[r, which],
             recv_sem=q_recv.at[r, which],
             device_id=(to, z, ha),
@@ -259,74 +291,71 @@
 
     for r in range(1, npb):
         kv_copy(r).start()
-    for r in range(1, npb):
-        q_copy(r, 0).start()
-        q_copy(r, 1).start()
-
-    def chain(h, r, up):
-        source = z - h if up else z + h
-        piece = kv.at[source, partner(r)]
+
+    def chain(h, c, up):
+        piece = kv.at[z - h if up else z + h, c]
         send, recv = (up_send, up_recv) if up else (down_send, down_recv)
         return pltpu.make_async_remote_copy(
             src_ref=piece,
             dst_ref=piece,
-            send_sem=send.at[h, r],
-            recv_sem=recv.at[h, r],
+            send_sem=send.at[h, c],
+            recv_sem=recv.at[h, c],
             device_id=(pb, z + 1 if up else z - 1, ha),
             device_id_type=MESH,
         )
 
-    def arrived(h, r, up):
-        source = z - h if up else z + h
-        piece = kv.at[source, partner(r)]
-        recv = up_recv if up else down_recv
-        send = up_send if up else down_send
+    def arrived(h, c, up):
+        piece = kv.at[z - h if up else z + h, c]
+        send, recv = (up_send, up_recv) if up else (down_send, down_recv)
         pltpu.make_async_remote_copy(
             src_ref=piece,
             dst_ref=piece,
-            send_sem=send.at[h - 1, r],
-            recv_sem=recv.at[h - 1, r],
+            send_sem=send.at[h - 1, c],
+            recv_sem=recv.at[h - 1, c],
             device_id=(pb, z - 1 if up else z + 1, ha),
             device_id_type=MESH,
         ).wait_recv()
 
-    def first_hop():
-        for r in range(npb):
-            if r > 0:
-                kv_copy(r).wait_recv()
+    for r in range(npb):
+        if r > 0:
+            kv_copy(r).wait_recv()
+
+        @pl.when(z < nkv - 1)
+        def _():
+            chain(0, partner(r), True).start()
+
+        @pl.when((z > 0) & (partner(r) < npb - 1))
+        def _():
+            chain(0, partner(r), False).start()
+
+    for r in range(1, npb):
+        q_copy(r, 0).start()
+        q_copy(r, 1).start()
+
+    def next_hop(h, c):
+        @pl.when(z - h >= 0)
+        def _():
+            arrived(h, c, True)
 
             @pl.when(z < nkv - 1)
             def _():
-                chain(0, r, True).start()
-
-            @pl.when(z > 0)
-            def _():
-                chain(0, r, False).start()
-
-    def next_hop(h):
-        for r in range(npb):
-
-            @pl.when(z - h >= 0)
-            def _():
-                arrived(h, r, True)
-
-                @pl.when(z < nkv - 1)
-                def _():
-                    chain(h, r, True).start()
+                chain(h, c, True).start()
+
+        if c < npb - 1:
 
             @pl.when(z + h <= nkv - 1)
             def _():
-                arrived(h, r, False)
+                arrived(h, c, False)
 
                 @pl.when(z > 0)
                 def _():
-                    chain(h, r, False).start()
-
-    first_hop()
-    next_hop(1)
-
-    tq_in[pb] = tq_ref[:, pl.ds(pl.multiple_of(pb * heads * TD, heads * TD), heads * TD)]
-    sq_in[pb] = sq_ref[:, pl.ds(pl.multiple_of(pb * heads * SD, heads * SD), heads * SD)]
+                    chain(h, c, False).start()
+
+    for c in range(npb):
+        next_hop(1, c)
+
+    for load in loads[5:]:
+        load.wait()
     for r in range(1, npb):
         q_copy(r, 0).wait_recv()
         q_copy(r, 1).wait_recv()
@@ -345,74 +374,69 @@
     local_key = lax.broadcasted_iota(jnp.int32, (rows, wide), 0)
     local_query = lax.broadcasted_iota(jnp.int32, (1, wide), 1) % rows
 
-    def attend(source):
-        firsts = []
-        for c in range(npb):
+    def attend(source, p, count):
+        keys = count * rows
+        own = kv[z, p, 3 * rows : 3 * rows + 16, :].astype(jnp.float32)[0:1, :]
+        query_doc = jnp.concatenate([own] * heads, axis=1)
+        allowed = []
+        for c in range(count):
             key_doc = kv[source, c, 3 * rows : 3 * rows + 16, :].astype(jnp.float32)[0:1, :]
-            firsts.append(
+            least = jnp.zeros((1, wide), jnp.float32)
+            for d in range(1, DOCS):
+                before = jnp.sum((key_doc < d).astype(jnp.float32), axis=1, keepdims=True)
+                least = jnp.where(query_doc == d, before, least)
+            ok = local_key >= least.astype(jnp.int32)
+            if c == p:
+                ok = ok & (local_key <= local_query + (z - source) * rows)
+            allowed.append(ok)
+        for which in range(2):
+            factor = math.log2(math.e) / math.sqrt((TD, SD)[which])
+            queries = (tq_all, sq_all)[which][p]
+            if which == 0:
+                key_rows = kv[source, 0:count, 0:rows, :].reshape(keys, TD)
+                value_rows = kv[source, 0:count, rows : 2 * rows, :].reshape(keys, TD)
+            else:
+                key_rows = kv[source, 0:count, 2 * rows : 3 * rows, :].reshape(keys, TD)
+                value_rows = key_rows
+            raw = rows_dot(key_rows, queries)
+            scores = jnp.concatenate(
                 [
-                    jnp.sum((key_doc < d).astype(jnp.float32), axis=1, keepdims=True)
-                    for d in range(1, DOCS)
-                ]
+                    jnp.where(allowed[c], raw[c * rows : (c + 1) * rows], NEGATIVE)
+                    for c in range(count)
+                ],
+                axis=0,
             )
+            old = soft[p, which : which + 1, :]
+            new = jnp.maximum(old, jnp.max(scores, axis=0, keepdims=True))
+            weights = jnp.exp2((scores - new) * factor)
+            shrink = jnp.exp2((old - new) * factor)
+            soft[p, which : which + 1, :] = new
+            soft[p, which + 2 : which + 3, :] = soft[
+                p, which + 2 : which + 3, :
+            ] * shrink + jnp.sum(weights, axis=0, keepdims=True)
+            mixed = columns_dot(value_rows, weights.astype(jnp.bfloat16))
+            if which == 0:
+                t_acc[p] = t_acc[p] * shrink + mixed
+            else:
+                s_acc[p] = s_acc[p] * shrink + mixed[TD - SD :]
+
+    def turn(h, carry):
         for p in range(npb):
-            keys = (p + 1) * rows
-            own = kv[z, p, 3 * rows : 3 * rows + 16, :].astype(jnp.float32)[0:1, :]
-            query_doc = jnp.concatenate([own] * heads, axis=1)
-            allowed = []
-            for c in range(p + 1):
-                least = jnp.zeros((1, wide), jnp.float32)
-                for d in range(1, DOCS):
-                    least = jnp.where(query_doc == d, firsts[c][d - 1], least)
-                ok = local_key >= least.astype(jnp.int32)
-                if c == p:
-                    ok = ok & (local_key <= local_query + (z - source) * rows)
-                allowed.append(ok)
-            for which in range(2):
-                size = (TD, SD)[which]
-                factor = math.log2(math.e) / math.sqrt(size)
-                queries = (tq_all, sq_all)[which][p]
-                if which == 0:
-                    key_rows = kv[source, 0 : p + 1, 0:rows, :].reshape(keys, TD)
-                    value_rows = kv[source, 0 : p + 1, rows : 2 * rows, :].reshape(keys, TD)
-                else:
-                    key_rows = kv[source, 0 : p + 1, 2 * rows : 3 * rows, :].reshape(keys, TD)
-                    value_rows = key_rows
-                raw = rows_dot(key_rows, queries) * factor
-                scores = jnp.concatenate(
-                    [
-                        jnp.where(allowed[c], raw[c * rows : (c + 1) * rows], NEGATIVE)
-                        for c in range(p + 1)
-                    ],
-                    axis=0,
-                )
-                old = soft[p, which : which + 1, :]
-                new = jnp.maximum(old, jnp.max(scores, axis=0, keepdims=True))
-                weights = jnp.exp2(scores - new)
-                shrink = jnp.exp2(old - new)
-                soft[p, which : which + 1, :] = new
-                soft[p, which + 2 : which + 3, :] = soft[
-                    p, which + 2 : which + 3, :
-                ] * shrink + jnp.sum(weights, axis=0, keepdims=True)
-                mixed = columns_dot(value_rows, weights.astype(jnp.bfloat16))
-                if which == 0:
-                    t_acc[p] = t_acc[p] * shrink + mixed
-                else:
-                    s_acc[p] = s_acc[p] * shrink + mixed[TD - SD :]
-
-    def turn(h, carry):
-        @pl.when(h >= 2)
-        def _():
-            next_hop(h)
-
-        below = (z - h >= 0).astype(jnp.int32)
-        above = ((z + h <= nkv - 1) & (h > 0)).astype(jnp.int32)
-
-        def visit(i, inner):
-            attend(jnp.where((i == 0) & (below == 1), z - h, z + h))
-            return inner
-
-        lax.fori_loop(0, below + above, visit, 0)
+
+            @pl.when(h >= 2)
+            def _():
+                next_hop(h, p)
+
+            @pl.when(z - h >= 0)
+            def _():
+                attend(z - h, p, p + 1)
+
+            if p > 0:
+
+                @pl.when((z + h <= nkv - 1) & (h > 0))
+                def _():
+                    attend(z + h, p, p)
+
         return carry
 
     lax.fori_loop(0, nkv, turn, 0)
@@ -458,7 +482,6 @@
     s_scale = lax.rsqrt(sums[npb : 2 * npb] * (1.0 / (heads * plane * SD)) + EPSILON)
 
     loss = jnp.zeros((1, npb * rows), jnp.float32)
-    first_head = (ha * npb + pb) * heads
     features, differences = [], []
     for j in range(heads):
         cut = slice(j * rows, (j + 1) * rows)
@@ -468,7 +491,7 @@
         feature = jnp.concatenate(
             [s_acc[p, :, cut] * s_scale[p : p + 1] for p in range(npb)], axis=1
         ).astype(jnp.bfloat16)
-        difference = columns_dot(w_ref[first_head + j], feature) - target
+        difference = columns_dot(w_ref[j], feature) - target
         loss = loss + jnp.sum(difference * difference, axis=0, keepdims=True)
         features.append(feature)
         differences.append(difference)
@@ -539,15 +562,17 @@
         q_copy(r, 0).wait_send()
         q_copy(r, 1).wait_send()
     for h in range(nkv - 1):
-        for r in range(npb):
+        for c in range(npb):
 
             @pl.when((z - h >= 0) & (z < nkv - 1))
             def _():
-                chain(h, r, True).wait_send()
-
-            @pl.when((z + h <= nkv - 1) & (z > 0))
-            def _():
-                chain(h, r, False).wait_send()
+                chain(h, c, True).wait_send()
+
+            if c < npb - 1:
+
+                @pl.when((z + h <= nkv - 1) & (z > 0))
+                def _():
+                    chain(h, c, False).wait_send()
 
     for r in range(1, plane):
         share(stats, stat_send, stat_recv, r).wait_send()
@@ -576,9 +601,15 @@
             jax.ShapeDtypeStruct((SD, TD), f32),
             jax.ShapeDtypeStruct((1, rows // nha), f32),
         ),
-        in_specs=[vmem] * 8,
+        in_specs=[pl.BlockSpec(memory_space=pltpu.HBM)] * 8,
         out_specs=(vmem, vmem),
         scratch_shapes=[
+            pltpu.VMEM(teacher_k.shape, bf16),
+            pltpu.VMEM(teacher_v.shape, bf16),
+            pltpu.VMEM(student_k.shape, bf16),
+            pltpu.VMEM(student_v.shape, bf16),
+            pltpu.VMEM((1, rows), jnp.int32),
+            pltpu.VMEM((heads, SD, TD), bf16),
             pltpu.VMEM((npb, 3 * rows + 16, TD), bf16),
             pltpu.VMEM((nkv, npb, 3 * rows + 16, TD), bf16),
             pltpu.VMEM((npb, rows, heads * TD), bf16),
@@ -606,9 +637,10 @@
             dma((plane,)),
             dma((heads,)),
             dma((nkv,)),
+            dma((8,)),
         ],
         compiler_params=pltpu.CompilerParams(
-            collective_id=0, has_side_effects=True, vmem_limit_bytes=48 * 1024 * 1024
+            collective_id=0, has_side_effects=True, vmem_limit_bytes=63 * 1024 * 1024
         ),
         name="attention_distillation",
     )(

time: 64.9 us -> 58.3 us (0.90)
  local copies, waits for them, and re-layouts: 8.29 us -> 1.89 us
    unnamed x18 -> x4, local copies, waits for them, and re-layouts: 8.29 us -> 1.89 us
where the time goes in v2:
time: 58.3 us; the launch traced here: 58.1 us
  Pallas kernels  55.5 us (95%)
  local copies, waits for them, and re-layouts  1.89 us (3%)
  between operations  0.65 us (1%)
    pallas_call x1, Pallas kernels, by_heads(): pl.pallas_call(functools.partial(fused, shape, rows * npb * nkv), out_sha...  55.5 us
    unnamed x4, local copies, waits for them, and re-layouts  1.89 us

profile of v2, /device:TPU:1, one launch (start us, length us, event | category | flops | bytes accessed | tf_op | source)
XLA Modules:
  0.0 58.1 jit_solution(14471568599155358384)
XLA Ops:
  0.6 55.5 %attention_distillation.1 = (f32[64,128]{1,0:T(8,128)}, f32[1,64]{1,0:T(1,128)}) custom-call(bf16[128,2048]{1,0:T(8,128)(2,1)} %tq_ref.1, bf16[128,512]{1,0:T(8,128)(2,1)} %tk_hbm.1, bf16[128,512]{1,0:T(8,128)(2,1)} %tv_hbm.1, bf16[128,1024]{1,0:T(8,128)(2,1)} %sq_ref.1, bf16[128,256]{1,0:T(8,128)(2,1)} %sk_hbm.1, bf16[128,256]{1,0:T(8,128)(2,1)} %sv_hbm.1, ...), custom_call_target="tpu_custom_call" | custom-call | tf_op jit(solution)/shard_map/attention_distillation/pallas_call | solution.py:598
  56.1 0.0 copy-start
  56.2 1.4 %copy.12 = f32[64,128]{1,0:T(8,128)} copy(f32[64,128]{1,0:T(8,128)} %get-tuple-element.8) | data formatting | bytes 65536
  57.5 0.0 copy-done
  57.5 0.5 copy.13
Async XLA Ops:
  56.1 1.4 %copy-start = (f32[1,64]{1,0:T(1,128)S(1)}, f32[1,64]{1,0:T(1,128)}, u32[]{:S(2)}) copy-start(f32[1,64]{1,0:T(1,128)} %get-tuple-element.5) | copy-start | bytes 772

commit v3 on v2

--- a/solution.py
+++ b/solution.py
@@ -255,7 +255,9 @@
     doc_rows = jnp.broadcast_to(doc_ref[...].astype(jnp.float32), (16, rows)).astype(jnp.bfloat16)
     for g in range(npb):
         stage[g, 0:rows, :] = tk_ref[:, g * TD : (g + 1) * TD]
-        stage[g, rows : 2 * rows, :] = tv_ref[:, g * TD : (g + 1) * TD]
+        stage[g, rows : 2 * rows, :] = (
+            tv_ref[:, g * TD : (g + 1) * TD].astype(jnp.float32).T.astype(jnp.bfloat16)
+        )
         stage[g, 2 * rows : 3 * rows, :] = jnp.concatenate(
             [sk_ref[:, g * SD : (g + 1) * SD], sv_ref[:, g * SD : (g + 1) * SD]], axis=1
         )
@@ -341,9 +343,9 @@
             def _():
                 chain(h, c, True).start()
 
-        if c < npb - 1:
-
-            @pl.when(z + h <= nkv - 1)
+        if not isinstance(c, int) or c < npb - 1:
+
+            @pl.when((z + h <= nkv - 1) & (c < npb - 1))
             def _():
                 arrived(h, c, False)
 
@@ -351,21 +353,6 @@
                 def _():
                     chain(h, c, False).start()
 
-    for c in range(npb):
-        next_hop(1, c)
-
-    for load in loads[5:]:
-        load.wait()
-    for r in range(1, npb):
-        q_copy(r, 0).wait_recv()
-        q_copy(r, 1).wait_recv()
-    blank = jnp.zeros((rows, TD - SD), jnp.bfloat16)
-    for p in range(npb):
-        for j in range(heads):
-            tq_all[p, j * rows : (j + 1) * rows, :] = tq_in[p, :, j * TD : (j + 1) * TD]
-            sq_all[p, j * rows : (j + 1) * rows, :] = jnp.concatenate(
-                [sq_in[p, :, j * SD : (j + 1) * SD], blank], axis=1
-            )
     t_acc[...] = jnp.zeros_like(t_acc)
     s_acc[...] = jnp.zeros_like(s_acc)
     soft[:, 0:2, :] = jnp.full((npb, 2, wide), NEGATIVE, jnp.float32)
@@ -373,35 +360,40 @@
 
     local_key = lax.broadcasted_iota(jnp.int32, (rows, wide), 0)
     local_query = lax.broadcasted_iota(jnp.int32, (1, wide), 1) % rows
-
-    def attend(source, p, count):
+    float_key = local_key.astype(jnp.float32)
+    float_query = local_query.astype(jnp.float32)
+
+    def attend(source, p, count, own_place=False):
         keys = count * rows
         own = kv[z, p, 3 * rows : 3 * rows + 16, :].astype(jnp.float32)[0:1, :]
         query_doc = jnp.concatenate([own] * heads, axis=1)
-        allowed = []
+        firsts = []
         for c in range(count):
             key_doc = kv[source, c, 3 * rows : 3 * rows + 16, :].astype(jnp.float32)[0:1, :]
             least = jnp.zeros((1, wide), jnp.float32)
             for d in range(1, DOCS):
                 before = jnp.sum((key_doc < d).astype(jnp.float32), axis=1, keepdims=True)
                 least = jnp.where(query_doc == d, before, least)
-            ok = local_key >= least.astype(jnp.int32)
-            if c == p:
-                ok = ok & (local_key <= local_query + (z - source) * rows)
-            allowed.append(ok)
+            firsts.append(least)
+
+        def allowed(c, which):
+            if which == 0:
+                ok = local_key >= firsts[c].astype(jnp.int32)
+                return ok & (local_key <= local_query) if own_place and c == p else ok
+            ok = float_key > firsts[c] - 0.5
+            return ok & (float_key < float_query + 0.5) if own_place and c == p else ok
+
         for which in range(2):
             factor = math.log2(math.e) / math.sqrt((TD, SD)[which])
             queries = (tq_all, sq_all)[which][p]
             if which == 0:
                 key_rows = kv[source, 0:count, 0:rows, :].reshape(keys, TD)
-                value_rows = kv[source, 0:count, rows : 2 * rows, :].reshape(keys, TD)
             else:
                 key_rows = kv[source, 0:count, 2 * rows : 3 * rows, :].reshape(keys, TD)
-                value_rows = key_rows
             raw = rows_dot(key_rows, queries)
             scores = jnp.concatenate(
                 [
-                    jnp.where(allowed[c], raw[c * rows : (c + 1) * rows], NEGATIVE)
+                    jnp.where(allowed(c, which), raw[c * rows : (c + 1) * rows], NEGATIVE)
                     for c in range(count)
                 ],
                 axis=0,
@@ -414,11 +406,44 @@
             soft[p, which + 2 : which + 3, :] = soft[
                 p, which + 2 : which + 3, :
             ] * shrink + jnp.sum(weights, axis=0, keepdims=True)
-            mixed = columns_dot(value_rows, weights.astype(jnp.bfloat16))
+            rounded = weights.astype(jnp.bfloat16)
             if which == 0:
-                t_acc[p] = t_acc[p] * shrink + mixed
+                values = jnp.concatenate(
+                    [kv[source, c, rows : 2 * rows, :] for c in range(count)], axis=1
+                )
+                t_acc[p] = t_acc[p] * shrink + jnp.dot(
+                    values, rounded, preferred_element_type=jnp.float32
+                )
             else:
-                s_acc[p] = s_acc[p] * shrink + mixed[TD - SD :]
+                s_acc[p] = s_acc[p] * shrink + columns_dot(key_rows, rounded)[TD - SD :]
+
+    for load in loads[5:]:
+        load.wait()
+    blank = jnp.zeros((rows, TD - SD), jnp.bfloat16)
+
+    def own_turn(r, carry):
+        place = partner(r)
+        next_hop(1, place)
+
+        @pl.when(r > 0)
+        def _():
+            q_copy(r, 0).wait_recv()
+            q_copy(r, 1).wait_recv()
+
+        for j in range(heads):
+            tq_all[place, j * rows : (j + 1) * rows, :] = tq_in[place, :, j * TD : (j + 1) * TD]
+            sq_all[place, j * rows : (j + 1) * rows, :] = jnp.concatenate(
+                [sq_in[place, :, j * SD : (j + 1) * SD], blank], axis=1
+            )
+        for p in range(npb):
+
+            @pl.when(place == p)
+            def _():
+                attend(z, p, p + 1, True)
+
+        return carry
+
+    lax.fori_loop(0, npb, own_turn, 0)
 
     def turn(h, carry):
         for p in range(npb):
@@ -433,13 +458,13 @@
 
             if p > 0:
 
-                @pl.when((z + h <= nkv - 1) & (h > 0))
+                @pl.when(z + h <= nkv - 1)
                 def _():
                     attend(z + h, p, p)
 
         return carry
 
-    lax.fori_loop(0, nkv, turn, 0)
+    lax.fori_loop(1, nkv, turn, 0)
 
     def by_token(row):
         total = row[:, 0:rows]

time: 58.3 us -> 54.4 us (0.933)
  Pallas kernels: 55.5 us -> 51.6 us
    pallas_call x1, Pallas kernels: 55.5 us -> 51.6 us  [by_heads(): pl.pallas_call(functools.partial(fused, shape, rows * npb * nkv), out_sha...]
where the time goes in v3:
time: 54.4 us; the launch traced here: 54.2 us
  Pallas kernels  51.6 us (95%)
  local copies, waits for them, and re-layouts  1.89 us (3%)
  between operations  0.65 us (1%)
    pallas_call x1, Pallas kernels, by_heads(): pl.pallas_call(functools.partial(fused, shape, rows * npb * nkv), out_sha...  51.6 us
    unnamed x4, local copies, waits for them, and re-layouts  1.89 us

profile of v3, /device:TPU:1, one launch (start us, length us, event | category | flops | bytes accessed | tf_op | source)
XLA Modules:
  0.0 54.2 jit_solution(11719586706599067884)
XLA Ops:
  0.6 51.6 %attention_distillation.1 = (f32[64,128]{1,0:T(8,128)}, f32[1,64]{1,0:T(1,128)}) custom-call(bf16[128,2048]{1,0:T(8,128)(2,1)} %tq_ref.1, bf16[128,512]{1,0:T(8,128)(2,1)} %tk_hbm.1, bf16[128,512]{1,0:T(8,128)(2,1)} %tv_hbm.1, bf16[128,1024]{1,0:T(8,128)(2,1)} %sq_ref.1, bf16[128,256]{1,0:T(8,128)(2,1)} %sk_hbm.1, bf16[128,256]{1,0:T(8,128)(2,1)} %sv_hbm.1, ...), custom_call_target="tpu_custom_call" | custom-call | tf_op jit(solution)/shard_map/attention_distillation/pallas_call | solution.py:623
  52.3 0.0 copy-start
  52.3 1.4 %copy.12 = f32[64,128]{1,0:T(8,128)} copy(f32[64,128]{1,0:T(8,128)} %get-tuple-element.8) | data formatting | bytes 65536
  53.7 0.0 copy-done
  53.7 0.5 copy.13
Async XLA Ops:
  52.3 1.4 %copy-start = (f32[1,64]{1,0:T(1,128)S(1)}, f32[1,64]{1,0:T(1,128)}, u32[]{:S(2)}) copy-start(f32[1,64]{1,0:T(1,128)} %get-tuple-element.5) | copy-start | bytes 772

commit v4 on v3

--- a/solution.py
+++ b/solution.py
@@ -363,8 +363,7 @@
     float_key = local_key.astype(jnp.float32)
     float_query = local_query.astype(jnp.float32)
 
-    def attend(source, p, count, own_place=False):
-        keys = count * rows
+    def masked_scores(source, p, count, own_place):
         own = kv[z, p, 3 * rows : 3 * rows + 16, :].astype(jnp.float32)[0:1, :]
         query_doc = jnp.concatenate([own] * heads, axis=1)
         firsts = []
@@ -383,43 +382,58 @@
             ok = float_key > firsts[c] - 0.5
             return ok & (float_key < float_query + 0.5) if own_place and c == p else ok
 
+        result = []
         for which in range(2):
-            factor = math.log2(math.e) / math.sqrt((TD, SD)[which])
-            queries = (tq_all, sq_all)[which][p]
-            if which == 0:
-                key_rows = kv[source, 0:count, 0:rows, :].reshape(keys, TD)
-            else:
-                key_rows = kv[source, 0:count, 2 * rows : 3 * rows, :].reshape(keys, TD)
-            raw = rows_dot(key_rows, queries)
-            scores = jnp.concatenate(
-                [
-                    jnp.where(allowed(c, which), raw[c * rows : (c + 1) * rows], NEGATIVE)
-                    for c in range(count)
-                ],
-                axis=0,
+            cut = slice(0, rows) if which == 0 else slice(2 * rows, 3 * rows)
+            key_rows = kv[source, 0:count, cut, :].reshape(count * rows, TD)
+            raw = rows_dot(key_rows, (tq_all, sq_all)[which][p])
+            result.append(
+                jnp.concatenate(
+                    [
+                        jnp.where(allowed(c, which), raw[c * rows : (c + 1) * rows], NEGATIVE)
+                        for c in range(count)
+                    ],
+                    axis=0,
+                )
             )
-            old = soft[p, which : which + 1, :]
-            new = jnp.maximum(old, jnp.max(scores, axis=0, keepdims=True))
-            weights = jnp.exp2((scores - new) * factor)
-            shrink = jnp.exp2((old - new) * factor)
-            soft[p, which : which + 1, :] = new
-            soft[p, which + 2 : which + 3, :] = soft[
-                p, which + 2 : which + 3, :
-            ] * shrink + jnp.sum(weights, axis=0, keepdims=True)
-            rounded = weights.astype(jnp.bfloat16)
-            if which == 0:
-                values = jnp.concatenate(
-                    [kv[source, c, rows : 2 * rows, :] for c in range(count)], axis=1
-                )
-                t_acc[p] = t_acc[p] * shrink + jnp.dot(
-                    values, rounded, preferred_element_type=jnp.float32
-                )
-            else:
-                s_acc[p] = s_acc[p] * shrink + columns_dot(key_rows, rounded)[TD - SD :]
+        return result
+
+    def absorb(source, p, count, which, scores):
+        factor = 1.0 / math.sqrt(TD) if which == 0 else 1.0
+        old = soft[p, which : which + 1, :]
+        new = jnp.maximum(old, jnp.max(scores, axis=0, keepdims=True))
+        weights = jnp.exp((scores - new) * factor)
+        shrink = jnp.exp((old - new) * factor)
+        soft[p, which : which + 1, :] = new
+        soft[p, which + 2 : which + 3, :] = soft[
+            p, which + 2 : which + 3, :
+        ] * shrink + jnp.sum(weights, axis=0, keepdims=True)
+        rounded = weights.astype(jnp.bfloat16)
+        if which == 0:
+            values = jnp.concatenate(
+                [kv[source, c, rows : 2 * rows, :] for c in range(count)], axis=1
+            )
+            t_acc[p] = t_acc[p] * shrink + jnp.dot(
+                values, rounded, preferred_element_type=jnp.float32
+            )
+        else:
+            key_rows = kv[source, 0:count, 2 * rows : 3 * rows, :].reshape(count * rows, TD)
+            s_acc[p] = s_acc[p] * shrink + columns_dot(key_rows, rounded)[TD - SD :]
+
+    def attend(source, pairs, own_place=False):
+        scores = masked_scores(source, *pairs[0], own_place)
+        for i, (p, count) in enumerate(pairs):
+            later = None
+            if i + 1 < len(pairs):
+                later = masked_scores(source, *pairs[i + 1], own_place)
+            for which in range(2):
+                absorb(source, p, count, which, scores[which])
+            scores = later
 
     for load in loads[5:]:
         load.wait()
     blank = jnp.zeros((rows, TD - SD), jnp.bfloat16)
+    scale = jnp.asarray(1.0 / math.sqrt(SD), jnp.bfloat16)
 
     def own_turn(r, carry):
         place = partner(r)
@@ -433,34 +447,41 @@
         for j in range(heads):
             tq_all[place, j * rows : (j + 1) * rows, :] = tq_in[place, :, j * TD : (j + 1) * TD]
             sq_all[place, j * rows : (j + 1) * rows, :] = jnp.concatenate(
-                [sq_in[place, :, j * SD : (j + 1) * SD], blank], axis=1
+                [sq_in[place, :, j * SD : (j + 1) * SD] * scale, blank], axis=1
             )
         for p in range(npb):
 
             @pl.when(place == p)
             def _():
-                attend(z, p, p + 1, True)
+                attend(z, [(p, p + 1)], True)
 
         return carry
 
     lax.fori_loop(0, npb, own_turn, 0)
 
-    def turn(h, carry):
-        for p in range(npb):
+    def hops(h, pieces):
+        for c in pieces:
 
             @pl.when(h >= 2)
             def _():
-                next_hop(h, p)
-
-            @pl.when(z - h >= 0)
-            def _():
-                attend(z - h, p, p + 1)
-
-            if p > 0:
-
-                @pl.when(z + h <= nkv - 1)
-                def _():
-                    attend(z + h, p, p)
+                next_hop(h, c)
+
+    def turn(h, carry):
+        hops(h, range(npb - 1))
+
+        @pl.when(z - h >= 0)
+        def _():
+            attend(z - h, [(p, p + 1) for p in range(npb - 1)])
+
+        hops(h, range(npb - 1, npb))
+
+        @pl.when(z - h >= 0)
+        def _():
+            attend(z - h, [(npb - 1, npb)])
+
+        @pl.when(z + h <= nkv - 1)
+        def _():
+            attend(z + h, [(p, p) for p in range(1, npb)])
 
         return carry
 

time: 54.4 us -> 54.1 us (level)
  no operation moved by 1% of the time
where the time goes in v4:
time: 54.1 us; the launch traced here: 53.9 us
  Pallas kernels  51.4 us (95%)
  local copies, waits for them, and re-layouts  1.89 us (3%)
  between operations  0.65 us (1%)
    pallas_call x1, Pallas kernels, by_heads(): pl.pallas_call(functools.partial(fused, shape, rows * npb * nkv), out_sha...  51.4 us
    unnamed x4, local copies, waits for them, and re-layouts  1.89 us

profile of v4, /device:TPU:1, one launch (start us, length us, event | category | flops | bytes accessed | tf_op | source)
XLA Modules:
  0.0 53.9 jit_solution(1465358702755638807)
XLA Ops:
  0.6 51.4 %attention_distillation.1 = (f32[64,128]{1,0:T(8,128)}, f32[1,64]{1,0:T(1,128)}) custom-call(bf16[128,2048]{1,0:T(8,128)(2,1)} %tq_ref.1, bf16[128,512]{1,0:T(8,128)(2,1)} %tk_hbm.1, bf16[128,512]{1,0:T(8,128)(2,1)} %tv_hbm.1, bf16[128,1024]{1,0:T(8,128)(2,1)} %sq_ref.1, bf16[128,256]{1,0:T(8,128)(2,1)} %sk_hbm.1, bf16[128,256]{1,0:T(8,128)(2,1)} %sv_hbm.1, ...), custom_call_target="tpu_custom_call" | custom-call | tf_op jit(solution)/shard_map/attention_distillation/pallas_call | solution.py:644
  52.0 0.0 copy-start
  52.0 1.4 %copy.12 = f32[64,128]{1,0:T(8,128)} copy(f32[64,128]{1,0:T(8,128)} %get-tuple-element.8) | data formatting | bytes 65536
  53.4 0.0 copy-done
  53.4 0.5 copy.13
Async XLA Ops:
  52.0 1.4 %copy-start = (f32[1,64]{1,0:T(1,128)S(1)}, f32[1,64]{1,0:T(1,128)}, u32[]{:S(2)}) copy-start(f32[1,64]{1,0:T(1,128)} %get-tuple-element.5) | copy-start | bytes 772

commit v5 on v4

--- a/solution.py
+++ b/solution.py
@@ -437,7 +437,6 @@
 
     def own_turn(r, carry):
         place = partner(r)
-        next_hop(1, place)
 
         @pl.when(r > 0)
         def _():
@@ -455,29 +454,34 @@
             def _():
                 attend(z, [(p, p + 1)], True)
 
+        next_hop(1, place)
         return carry
 
     lax.fori_loop(0, npb, own_turn, 0)
 
-    def hops(h, pieces):
+    def hops(h, early, pieces):
         for c in pieces:
 
-            @pl.when(h >= 2)
+            @pl.when(((h >= 2) & (h <= nkv - 2)) if early else (h == nkv - 1))
             def _():
                 next_hop(h, c)
 
     def turn(h, carry):
-        hops(h, range(npb - 1))
+        hops(h + 1, True, range(1))
+        hops(h, False, range(npb - 1))
 
         @pl.when(z - h >= 0)
         def _():
             attend(z - h, [(p, p + 1) for p in range(npb - 1)])
 
-        hops(h, range(npb - 1, npb))
+        hops(h + 1, True, range(1, npb - 1))
+        hops(h, False, range(npb - 1, npb))
 
         @pl.when(z - h >= 0)
         def _():
             attend(z - h, [(npb - 1, npb)])
+
+        hops(h + 1, True, range(npb - 1, npb))
 
         @pl.when(z + h <= nkv - 1)
         def _():

time: 54.1 us -> 52.9 us (0.978)
  Pallas kernels: 51.4 us -> 50.1 us
    pallas_call x1, Pallas kernels: 51.4 us -> 50.1 us  [by_heads(): pl.pallas_call(functools.partial(fused, shape, rows * npb * nkv), out_sha...]
where the time goes in v5:
time: 52.9 us; the launch traced here: 52.7 us
  Pallas kernels  50.1 us (95%)
  local copies, waits for them, and re-layouts  1.89 us (4%)
  between operations  0.65 us (1%)
    pallas_call x1, Pallas kernels, by_heads(): pl.pallas_call(functools.partial(fused, shape, rows * npb * nkv), out_sha...  50.1 us
    unnamed x4, local copies, waits for them, and re-layouts  1.89 us

profile of v5, /device:TPU:1, one launch (start us, length us, event | category | flops | bytes accessed | tf_op | source)
XLA Modules:
  0.0 52.7 jit_solution(9089470901676915991)
XLA Ops:
  0.6 50.1 %attention_distillation.1 = (f32[64,128]{1,0:T(8,128)}, f32[1,64]{1,0:T(1,128)}) custom-call(bf16[128,2048]{1,0:T(8,128)(2,1)} %tq_ref.1, bf16[128,512]{1,0:T(8,128)(2,1)} %tk_hbm.1, bf16[128,512]{1,0:T(8,128)(2,1)} %tv_hbm.1, bf16[128,1024]{1,0:T(8,128)(2,1)} %sq_ref.1, bf16[128,256]{1,0:T(8,128)(2,1)} %sk_hbm.1, bf16[128,256]{1,0:T(8,128)(2,1)} %sv_hbm.1, ...), custom_call_target="tpu_custom_call" | custom-call | tf_op jit(solution)/shard_map/attention_distillation/pallas_call | solution.py:648
  50.8 0.0 copy-start
  50.8 1.4 %copy.12 = f32[64,128]{1,0:T(8,128)} copy(f32[64,128]{1,0:T(8,128)} %get-tuple-element.8) | data formatting | bytes 65536
  52.1 0.0 copy-done
  52.2 0.5 copy.13
Async XLA Ops:
  50.8 1.4 %copy-start = (f32[1,64]{1,0:T(1,128)S(1)}, f32[1,64]{1,0:T(1,128)}, u32[]{:S(2)}) copy-start(f32[1,64]{1,0:T(1,128)} %get-tuple-element.5) | copy-start | bytes 772

commit v6 on v5

--- a/solution.py
+++ b/solution.py
@@ -363,11 +363,11 @@
     float_key = local_key.astype(jnp.float32)
     float_query = local_query.astype(jnp.float32)
 
-    def masked_scores(source, p, count, own_place):
+    def masked_scores(source, p, first, last, own_place):
         own = kv[z, p, 3 * rows : 3 * rows + 16, :].astype(jnp.float32)[0:1, :]
         query_doc = jnp.concatenate([own] * heads, axis=1)
         firsts = []
-        for c in range(count):
+        for c in range(first, last):
             key_doc = kv[source, c, 3 * rows : 3 * rows + 16, :].astype(jnp.float32)[0:1, :]
             least = jnp.zeros((1, wide), jnp.float32)
             for d in range(1, DOCS):
@@ -377,28 +377,32 @@
 
         def allowed(c, which):
             if which == 0:
-                ok = local_key >= firsts[c].astype(jnp.int32)
+                ok = local_key >= firsts[c - first].astype(jnp.int32)
                 return ok & (local_key <= local_query) if own_place and c == p else ok
-            ok = float_key > firsts[c] - 0.5
+            ok = float_key > firsts[c - first] - 0.5
             return ok & (float_key < float_query + 0.5) if own_place and c == p else ok
 
         result = []
         for which in range(2):
             cut = slice(0, rows) if which == 0 else slice(2 * rows, 3 * rows)
-            key_rows = kv[source, 0:count, cut, :].reshape(count * rows, TD)
+            key_rows = kv[source, first:last, cut, :].reshape((last - first) * rows, TD)
             raw = rows_dot(key_rows, (tq_all, sq_all)[which][p])
             result.append(
                 jnp.concatenate(
                     [
-                        jnp.where(allowed(c, which), raw[c * rows : (c + 1) * rows], NEGATIVE)
-                        for c in range(count)
+                        jnp.where(
+                            allowed(c, which),
+                            raw[(c - first) * rows : (c - first + 1) * rows],
+                            NEGATIVE,
+                        )
+                        for c in range(first, last)
                     ],
                     axis=0,
                 )
             )
         return result
 
-    def absorb(source, p, count, which, scores):
+    def absorb(source, p, first, last, which, scores):
         factor = 1.0 / math.sqrt(TD) if which == 0 else 1.0
         old = soft[p, which : which + 1, :]
         new = jnp.maximum(old, jnp.max(scores, axis=0, keepdims=True))
@@ -411,23 +415,24 @@
         rounded = weights.astype(jnp.bfloat16)
         if which == 0:
             values = jnp.concatenate(
-                [kv[source, c, rows : 2 * rows, :] for c in range(count)], axis=1
+                [kv[source, c, rows : 2 * rows, :] for c in range(first, last)], axis=1
             )
             t_acc[p] = t_acc[p] * shrink + jnp.dot(
                 values, rounded, preferred_element_type=jnp.float32
             )
         else:
-            key_rows = kv[source, 0:count, 2 * rows : 3 * rows, :].reshape(count * rows, TD)
+            key_rows = kv[source, first:last, 2 * rows : 3 * rows, :]
+            key_rows = key_rows.reshape((last - first) * rows, TD)
             s_acc[p] = s_acc[p] * shrink + columns_dot(key_rows, rounded)[TD - SD :]
 
-    def attend(source, pairs, own_place=False):
-        scores = masked_scores(source, *pairs[0], own_place)
-        for i, (p, count) in enumerate(pairs):
+    def attend(source, blocks, own_place=False):
+        scores = masked_scores(source, *blocks[0], own_place)
+        for i, block in enumerate(blocks):
             later = None
-            if i + 1 < len(pairs):
-                later = masked_scores(source, *pairs[i + 1], own_place)
+            if i + 1 < len(blocks):
+                later = masked_scores(source, *blocks[i + 1], own_place)
             for which in range(2):
-                absorb(source, p, count, which, scores[which])
+                absorb(source, *block, which, scores[which])
             scores = later
 
     for load in loads[5:]:
@@ -452,7 +457,7 @@
 
             @pl.when(place == p)
             def _():
-                attend(z, [(p, p + 1)], True)
+                attend(z, [(p, 0, p + 1)], True)
 
         next_hop(1, place)
         return carry
@@ -472,20 +477,20 @@
 
         @pl.when(z - h >= 0)
         def _():
-            attend(z - h, [(p, p + 1) for p in range(npb - 1)])
+            attend(z - h, [(p, 0, min(p + 1, npb - 1)) for p in range(npb)])
 
         hops(h + 1, True, range(1, npb - 1))
         hops(h, False, range(npb - 1, npb))
 
         @pl.when(z - h >= 0)
         def _():
-            attend(z - h, [(npb - 1, npb)])
+            attend(z - h, [(npb - 1, npb - 1, npb)])
 
         hops(h + 1, True, range(npb - 1, npb))
 
         @pl.when(z + h <= nkv - 1)
         def _():
-            attend(z + h, [(p, p) for p in range(1, npb)])
+            attend(z + h, [(p, 0, p) for p in range(1, npb)])
 
         return carry
 
@@ -531,28 +536,6 @@
     t_scale = lax.rsqrt(sums[0:npb] * (1.0 / (heads * plane * TD)) + EPSILON)
     s_scale = lax.rsqrt(sums[npb : 2 * npb] * (1.0 / (heads * plane * SD)) + EPSILON)
 
-    loss = jnp.zeros((1, npb * rows), jnp.float32)
-    features, differences = [], []
-    for j in range(heads):
-        cut = slice(j * rows, (j + 1) * rows)
-        target = jnp.concatenate(
-            [t_acc[p, :, cut] * t_scale[p : p + 1] for p in range(npb)], axis=1
-        )
-        feature = jnp.concatenate(
-            [s_acc[p, :, cut] * s_scale[p : p + 1] for p in range(npb)], axis=1
-        ).astype(jnp.bfloat16)
-        difference = columns_dot(w_ref[j], feature) - target
-        loss = loss + jnp.sum(difference * difference, axis=0, keepdims=True)
-        features.append(feature)
-        differences.append(difference)
-    losses[slot] = jnp.concatenate(
-        [loss[:, p * rows : (p + 1) * rows] for p in range(npb)]
-        + [jnp.zeros((8 - npb, rows), jnp.float32)],
-        axis=0,
-    )
-    for r in range(1, plane):
-        share(losses, loss_send, loss_recv, r).start()
-
     def grad_copy(j):
         return pltpu.make_async_remote_copy(
             src_ref=grads.at[j],
@@ -563,10 +546,19 @@
             device_id_type=MESH,
         )
 
+    loss = jnp.zeros((1, npb * rows), jnp.float32)
     for j in range(heads):
-        high = differences[j].astype(jnp.bfloat16)
-        low = (differences[j] - high.astype(jnp.float32)).astype(jnp.bfloat16)
-        grads[j] = rows_dot(features[j], high) + rows_dot(features[j], low)
+        cut = slice(j * rows, (j + 1) * rows)
+        target = jnp.concatenate(
+            [t_acc[p, :, cut] * t_scale[p : p + 1] for p in range(npb)], axis=1
+        )
+        feature = jnp.concatenate(
+            [s_acc[p, :, cut] * s_scale[p : p + 1] for p in range(npb)], axis=1
+        ).astype(jnp.bfloat16)
+        difference = columns_dot(w_ref[j], feature) - target
+        high = difference.astype(jnp.bfloat16)
+        low = (difference - high.astype(jnp.float32)).astype(jnp.bfloat16)
+        grads[j] = rows_dot(feature, high) + rows_dot(feature, low)
 
         @pl.when(first_head + j != me)
         def _():
@@ -575,6 +567,15 @@
         @pl.when(first_head + j == me)
         def _():
             grads_in[z] = grads[j]
+
+        loss = loss + jnp.sum(difference * difference, axis=0, keepdims=True)
+    losses[slot] = jnp.concatenate(
+        [loss[:, p * rows : (p + 1) * rows] for p in range(npb)]
+        + [jnp.zeros((8 - npb, rows), jnp.float32)],
+        axis=0,
+    )
+    for r in range(1, plane):
+        share(losses, loss_send, loss_recv, r).start()
 
     for r in range(1, plane):
         share(losses, loss_send, loss_recv, r).wait_recv()

time: 52.9 us -> 53.1 us (level)
  no operation moved by 1% of the time
where the time goes in v6:
time: 53.1 us; the launch traced here: 52.8 us
  Pallas kernels  50.3 us (95%)
  local copies, waits for them, and re-layouts  1.89 us (4%)
  between operations  0.65 us (1%)
    pallas_call x1, Pallas kernels, by_heads(): pl.pallas_call(functools.partial(fused, shape, rows * npb * nkv), out_sha...  50.3 us
    unnamed x4, local copies, waits for them, and re-layouts  1.89 us

profile of v6, /device:TPU:1, one launch (start us, length us, event | category | flops | bytes accessed | tf_op | source)
XLA Modules:
  0.0 52.8 jit_solution(8008225753948438609)
XLA Ops:
  0.6 50.3 %attention_distillation.1 = (f32[64,128]{1,0:T(8,128)}, f32[1,64]{1,0:T(1,128)}) custom-call(bf16[128,2048]{1,0:T(8,128)(2,1)} %tq_ref.1, bf16[128,512]{1,0:T(8,128)(2,1)} %tk_hbm.1, bf16[128,512]{1,0:T(8,128)(2,1)} %tv_hbm.1, bf16[128,1024]{1,0:T(8,128)(2,1)} %sq_ref.1, bf16[128,256]{1,0:T(8,128)(2,1)} %sk_hbm.1, bf16[128,256]{1,0:T(8,128)(2,1)} %sv_hbm.1, ...), custom_call_target="tpu_custom_call" | custom-call | tf_op jit(solution)/shard_map/attention_distillation/pallas_call | solution.py:649
  50.9 0.0 copy-start
  51.0 1.4 %copy.12 = f32[64,128]{1,0:T(8,128)} copy(f32[64,128]{1,0:T(8,128)} %get-tuple-element.8) | data formatting | bytes 65536
  52.3 0.0 copy-done
  52.3 0.5 copy.13
Async XLA Ops:
  50.9 1.4 %copy-start = (f32[1,64]{1,0:T(1,128)S(1)}, f32[1,64]{1,0:T(1,128)}, u32[]{:S(2)}) copy-start(f32[1,64]{1,0:T(1,128)} %get-tuple-element.5) | copy-start | bytes 772

commit v7 on v5

--- a/solution.py
+++ b/solution.py
@@ -293,6 +293,9 @@
 
     for r in range(1, npb):
         kv_copy(r).start()
+    for r in range(1, npb):
+        q_copy(r, 0).start()
+        q_copy(r, 1).start()
 
     def chain(h, c, up):
         piece = kv.at[z - h if up else z + h, c]
@@ -329,10 +332,6 @@
         @pl.when((z > 0) & (partner(r) < npb - 1))
         def _():
             chain(0, partner(r), False).start()
-
-    for r in range(1, npb):
-        q_copy(r, 0).start()
-        q_copy(r, 1).start()
 
     def next_hop(h, c):
         @pl.when(z - h >= 0)

time: 52.9 us -> 52.1 us (0.985)
  Pallas kernels: 50.1 us -> 49.4 us
    pallas_call x1, Pallas kernels: 50.1 us -> 49.4 us  [by_heads(): pl.pallas_call(functools.partial(fused, shape, rows * npb * nkv), out_sha...]
where the time goes in v7:
time: 52.1 us; the launch traced here: 51.9 us
  Pallas kernels  49.4 us (95%)
  local copies, waits for them, and re-layouts  1.89 us (4%)
  between operations  0.65 us (1%)
    pallas_call x1, Pallas kernels, by_heads(): pl.pallas_call(functools.partial(fused, shape, rows * npb * nkv), out_sha...  49.4 us
    unnamed x4, local copies, waits for them, and re-layouts  1.89 us

profile of v7, /device:TPU:1, one launch (start us, length us, event | category | flops | bytes accessed | tf_op | source)
XLA Modules:
  0.0 51.9 jit_solution(17621520366748584291)
XLA Ops:
  0.6 49.4 %attention_distillation.1 = (f32[64,128]{1,0:T(8,128)}, f32[1,64]{1,0:T(1,128)}) custom-call(bf16[128,2048]{1,0:T(8,128)(2,1)} %tq_ref.1, bf16[128,512]{1,0:T(8,128)(2,1)} %tk_hbm.1, bf16[128,512]{1,0:T(8,128)(2,1)} %tv_hbm.1, bf16[128,1024]{1,0:T(8,128)(2,1)} %sq_ref.1, bf16[128,256]{1,0:T(8,128)(2,1)} %sk_hbm.1, bf16[128,256]{1,0:T(8,128)(2,1)} %sv_hbm.1, ...), custom_call_target="tpu_custom_call" | custom-call | tf_op jit(solution)/shard_map/attention_distillation/pallas_call | solution.py:647
  50.0 0.0 copy-start
  50.0 1.4 %copy.12 = f32[64,128]{1,0:T(8,128)} copy(f32[64,128]{1,0:T(8,128)} %get-tuple-element.8) | data formatting | bytes 65536
  51.4 0.0 copy-done
  51.4 0.5 copy.13
Async XLA Ops:
  50.0 1.4 %copy-start = (f32[1,64]{1,0:T(1,128)S(1)}, f32[1,64]{1,0:T(1,128)}, u32[]{:S(2)}) copy-start(f32[1,64]{1,0:T(1,128)} %get-tuple-element.5) | copy-start | bytes 772
